TPU v7x, 512 devices: a whole 4x8x8 slice. The times are simulated.
512 devices in a mesh: shot: 32 (over z_hi, x, core), sub: 16 (over z_lo, y).
Axes of the slice: x: 4, y: 8, z: 8 (z_hi: 4, z_lo: 2; z = z_hi * 2 + z_lo), core: 2. Of those that a mesh axis runs over, the one named last changes fastest.
Arguments:
- wave_before: bfloat16 [32, 128, 64, 128], P('shot', 'sub'), may hold values from -6 to 6
- wave_now: bfloat16 [32, 128, 64, 128], P('shot', 'sub'), may hold values from -6 to 6
- adjoint_before: bfloat16 [32, 128, 64, 128], P('shot', 'sub'), may hold values from -6 to 6
- adjoint_now: bfloat16 [32, 128, 64, 128], P('shot', 'sub'), may hold values from -6 to 6
- velocity: float32 [128, 64, 128], P('sub', 'shot'), may hold values from 0.06 to 0.19
- target_model: float32 [128, 64, 128], P('sub', 'shot'), may hold values from -0.8 to 1
- source_cell: int32 [32, 3], P('shot'), may hold values from 0 to 127, as said below
- source_wave: float32 [32, 2], P('shot'), may hold values from -12 to 12
- receiver_cell: int32 [32, 256, 2], P('shot'), may hold values from 0 to 127, as said below
- receiver_trace: float32 [32, 2, 256], P('shot'), may hold values from -10 to 10
- first_kernel: float32 [16, 2, 3, 3, 3], replicated, may hold values from -0.36 to 0.36
- first_bias: float32 [16], replicated, may hold values from -3 to 3
- second_kernel: float32 [1, 16, 3, 3, 3], replicated, may hold values from -0.9 to 0.9
- second_bias: float32 [1], replicated, may hold values from -4 to 4
Outputs:
- next_wave: bfloat16 [32, 128, 64, 128], P('shot', 'sub')
- new_velocity: float32 [128, 64, 128], P('sub', 'shot')
- first_kernel_move: float32 [16, 2, 3, 3, 3], replicated
- first_bias_move: float32 [16], replicated
- second_kernel_move: float32 [1, 16, 3, 3, 3], replicated
- second_bias_move: float32 [1], replicated
Inputs may be any that keep to these rules, and one draw needn't show every extreme that they name: `source_cell`: row s holds shot s's source cell: a first index below 128, a second below 64, a third below 128. `receiver_cell`: entry [s, r] holds receiver r of shot s: a first index below 128 and a second below 64; several receivers may share a cell.
All inputs are finite; a program needn't handle non-finite values.
Results may differ from a plain program's by a relative error of at most 0.001.
Values sent between devices are 32-bit elements; how exact they have to be, the bound alone decides.
A program may use at most 128 MiB of HBM per device.

v0:
```python
import jax
import jax.numpy as jnp
from jax import lax
from jax.sharding import PartitionSpec as P

STEPS = 2
ZREC = 2


COEFFS = (-205.0 / 72.0, 8.0 / 5.0, -1.0 / 5.0, 8.0 / 315.0, -1.0 / 560.0)
CENTER_SHIFT = 0.125
CENTER_GAIN = 16.0
NUMBERS = ("NCDHW", "OIDHW", "NCDHW")


def extended_2(cells, sides, width):
    for axis, dim in sides:
        count = lax.axis_size(axis)
        ends = count - 1
        head = lax.slice_in_dim(cells, 0, width, axis=dim)
        tail = lax.slice_in_dim(cells, cells.shape[dim] - width, cells.shape[dim], axis=dim)
        cells = jnp.concatenate(
            [
                lax.ppermute(tail, axis, [(i, (i + 1) % count) for i in range(ends)]),
                cells,
                lax.ppermute(head, axis, [((i + 1) % count, i) for i in range(ends)]),
            ],
            axis=dim,
        )
    return cells


def laplacian_inner(values):
    padded = jnp.pad(values, ((0, 0), (4, 4), (4, 4)))
    length = values.shape[0] - 8
    cols_y = values.shape[1]
    depth_z = values.shape[2]
    middle = padded[4 : 4 + length]
    running = 3.0 * COEFFS[0] * middle[:, 4 : 4 + cols_y, 4 : 4 + depth_z]
    for offset in range(1, 5):
        weight = COEFFS[offset]
        running = running + weight * (
            padded[4 + offset : 4 + offset + length, 4 : 4 + cols_y, 4 : 4 + depth_z]
            + padded[4 - offset : 4 - offset + length, 4 : 4 + cols_y, 4 : 4 + depth_z]
        )
        running = running + weight * (
            middle[:, 4 + offset : 4 + offset + cols_y, 4 : 4 + depth_z]
            + middle[:, 4 - offset : 4 - offset + cols_y, 4 : 4 + depth_z]
        )
        running = running + weight * (
            middle[:, 4 : 4 + cols_y, 4 + offset : 4 + offset + depth_z]
            + middle[:, 4 : 4 + cols_y, 4 - offset : 4 - offset + depth_z]
        )
    return running


def trim_rows(values, have_margin, want_margin):
    excess = have_margin - want_margin
    return values[excess : values.shape[0] - excess]


def wave_step(previous, prev_margin, current, cur_margin, model_ext, model_margin, inject, step):
    lap_now = laplacian_inner(current)
    out_margin = cur_margin - 4
    fresh = (
        2.0 * trim_rows(current, cur_margin, out_margin)
        - trim_rows(previous, prev_margin, out_margin)
        + trim_rows(model_ext, model_margin, out_margin) * lap_now
    )
    return (inject(fresh, out_margin, step), lap_now, out_margin)


def convolve(inputs, kernel, pads):
    return lax.conv_general_dilated(
        inputs, kernel, (1, 1, 1), pads, dimension_numbers=NUMBERS, precision=lax.Precision.HIGHEST
    )


def shards(
    wave_before,
    wave_now,
    adjoint_before,
    adjoint_now,
    velocity,
    target_model,
    source_cell,
    source_wave,
    receiver_cell,
    receiver_trace,
    first_kernel,
    first_bias,
    second_kernel,
    second_bias,
):
    rows_x = velocity.shape[0]
    rows_y = velocity.shape[1]
    depth_z = velocity.shape[2]
    shot_count = lax.axis_size("shot")
    sub_count = lax.axis_size("sub")
    model_full = lax.all_gather(velocity, "shot", axis=1, tiled=True)
    cols_y = model_full.shape[1]
    start_x = lax.axis_index("sub") * rows_x
    depth_iota = lax.iota(jnp.int32, depth_z)
    col_iota = lax.iota(jnp.int32, cols_y)
    receiver_marker = (depth_iota == ZREC).astype(jnp.float32)
    cell = source_cell[0]
    amplitudes = source_wave[0]
    rec_cells = receiver_cell[0]
    traces = receiver_trace[0]
    yz_marker = (col_iota == cell[1]).astype(jnp.float32)[:, None] * (depth_iota == cell[2]).astype(
        jnp.float32
    )[None, :]
    rec_y = (rec_cells[:, 1][:, None] == col_iota[None, :]).astype(jnp.float32)

    def x_positions(margin):
        return start_x - margin + lax.iota(jnp.int32, rows_x + 2 * margin)

    def add_source(fresh, margin, step):
        x_marker = (x_positions(margin) == cell[0]).astype(jnp.float32)
        return fresh + amplitudes[step] * (x_marker[:, None, None] * yz_marker[None, :, :])

    def add_receivers(fresh, margin, step):
        x_hits = (x_positions(margin)[:, None] == rec_cells[:, 0][None, :]).astype(
            jnp.float32
        ) * traces[step][None, :]
        surface = jnp.dot(x_hits, rec_y, precision=lax.Precision.HIGHEST)
        return fresh + surface[:, :, None] * receiver_marker[None, None, :]

    w_prev = wave_before[0].astype(jnp.float32)
    w_now = wave_now[0].astype(jnp.float32)
    a_prev = adjoint_before[0].astype(jnp.float32)
    a_now = adjoint_now[0].astype(jnp.float32)
    lap_list = []
    adjoint_list = []
    for step in range(STEPS):
        w_ext = extended_2(w_now, (("sub", 0),), 4)
        a_ext = extended_2(a_now, (("sub", 0),), 4)
        fresh, lap_now, new_margin = wave_step(w_prev, 0, w_ext, 4, model_full, 0, add_source, step)
        lap_list.append(lap_now)
        w_prev, w_now = (w_now, fresh)
        fresh, lap_adj, new_margin = wave_step(
            a_prev, 0, a_ext, 4, model_full, 0, add_receivers, step
        )
        adjoint_list.append(fresh)
        a_prev, a_now = (a_now, fresh)
    image_term = lap_list[0] * adjoint_list[STEPS - 1]
    step = 1
    image_term = image_term + lap_list[step] * adjoint_list[STEPS - 1 - step]
    image_piece = lax.psum_scatter(image_term, "shot", scatter_dimension=1, tiled=True) * (
        1.0 / shot_count
    )
    next_wave = w_now.astype(jnp.bfloat16)[None]
    centered = (velocity - CENTER_SHIFT) * CENTER_GAIN
    extended = extended_2(jnp.stack([image_piece, centered]), (("shot", 2), ("sub", 1)), 2)
    x_cells = x_positions(1)
    x_inside = ((x_cells >= 0) & (x_cells < rows_x * sub_count)).astype(jnp.float32)
    y_cells = lax.axis_index("shot") * rows_y - 1 + lax.iota(jnp.int32, rows_y + 2)
    y_inside = ((y_cells >= 0) & (y_cells < rows_y * shot_count)).astype(jnp.float32)
    inside = x_inside[:, None] * y_inside[None, :]

    def network(weights_one, offsets_one, weights_two, offsets_two):
        pre_act = (
            convolve(extended[None], weights_one, ((0, 0), (0, 0), (1, 1)))
            + offsets_one[None, :, None, None, None]
        )
        hidden = jnp.tanh(pre_act) * inside[None, None, :, :, None]
        update = convolve(hidden, weights_two, ((0, 0), (0, 0), (1, 1)))[0, 0] + offsets_two[0]
        new_model = velocity - update
        misfit = new_model - target_model
        return (0.5 * jnp.sum(misfit * misfit), new_model)

    loss_sum, pullback, new_velocity = jax.vjp(
        network, first_kernel, first_bias, second_kernel, second_bias, has_aux=True
    )
    local_terms = pullback(jnp.ones_like(loss_sum))
    gradients = lax.psum(
        (local_terms[0], local_terms[1], local_terms[2], local_terms[3]), ("shot", "sub")
    )
    square_sum = (
        jnp.sum(gradients[0] * gradients[0])
        + jnp.sum(gradients[1] * gradients[1])
        + jnp.sum(gradients[2] * gradients[2])
        + jnp.sum(gradients[3] * gradients[3])
    )
    entries = first_kernel.size + first_bias.size + second_kernel.size + second_bias.size
    factor = 1.0 / jnp.sqrt(square_sum / entries + 1e-06)
    return (
        next_wave,
        new_velocity,
        gradients[0] * factor,
        gradients[1] * factor,
        gradients[2] * factor,
        gradients[3] * factor,
    )


def solution(mesh):
    return jax.shard_map(
        shards,
        mesh=mesh,
        in_specs=(
            P("shot", "sub", None, None),
            P("shot", "sub", None, None),
            P("shot", "sub", None, None),
            P("shot", "sub", None, None),
            P("sub", "shot", None),
            P("sub", "shot", None),
            P("shot", None),
            P("shot", None),
            P("shot", None, None),
            P("shot", None, None),
            P(),
            P(),
            P(),
            P(),
        ),
        out_specs=(P("shot", "sub", None, None), P("sub", "shot", None), P(), P(), P(), P()),
        check_vma=False,
    )
```

profile of v0, /device:TPU:1, one launch (start us, length us, event | category | flops | bytes accessed | tf_op | source)
XLA Modules:
  0.0 529.0 jit_solution(17499774509085849016)
XLA Ops:
  8.4 1.3 collective-permute-start.4
  9.7 4.7 collective-permute-start.5
  14.5 3.5 collective-permute-start.1
  18.0 1.3 collective-permute-start
  23.3 52.1 %all_gather.3 = f32[8,64,128]{2,0,1:T(8,128)S(1)} all-gather(f32[8,2,128]{2,0,1:T(8,128)S(1)} %get-tuple-element.69), channel_id=1, replica_groups=mesh['shot'=32,'sub'=16] {'shot'}, dimensions={1}, use_global_device_ids=true | all-gather | bytes 270336 | tf_op jit(solution)/shard_map/all_gather | solution.py:100
  76.0 1.8 fusion.41
  77.9 4.3 collective-permute-start.3
  82.3 1.3 collective-permute-start.2
  85.4 1.3 collective-permute-start.6
  86.7 5.2 collective-permute-start.7
  95.0 3.3 fusion.57
  98.3 94.3 %reduce-scatter.2.cloned.1.call-done = f32[8,2,128]{2,0,1:T(8,128)} async-done(((f32[8,64,128]{2,0,1:T(8,128)}), f32[8,2,128]{2,0,1:T(8,128)}) %reduce-scatter.2.cloned.1.call-update) | async-done | bytes 8208 | tf_op jit(solution)/shard_map/reduce_scatter | solution.py:149
  193.3 4.5 collective-permute-start.9
  197.8 2.4 collective-permute-start.8
  201.1 3.1 collective-permute-start.10
  204.2 1.3 collective-permute-start.11
  207.0 1.7 collective-permute-done.11
  209.3 1.3 fusion.229
  214.1 31.8 %fusion.18 = f32[10,4,8,17,16]{4,2,3,1,0:T(8,128)S(1)} fusion(f32[16,2,3,3,3]{0,1,4,3,2:T(2,128)S(1)} %copy-done, f32[2,12,6,8,19]{3,0,4,2,1:T(2,128)S(1)} %fusion.247), kind=kOutput, calls=%fused_computation.32 | convolution fusion | flops 56401920 | bytes 439168 | tf_op jit(solution)/shard_map/jvp()/conv_general_dilated | solution.py:74
  246.0 2.4 fusion.14
  249.1 51.1 %fusion.23 = f32[8,2,8,17,1]{4,2,3,1,0:T(8,128)} fusion(f32[1,16,3,3,3]{1,0,4,3,2:T(1,128)S(1)} %copy-done.27, f32[10,4,1,8,1,16]{5,3,4,1,0,2:T(8,128)S(1)} %pad.20, f32[10,4,1,8,17,16]{5,3,4,1,0,2:T(8,128)S(1)} %get-tuple-element.41, f32[10,4,1,8,1,16]{5,3,4,1,0,2:T(8,128)S(1)} %pad.19, f32[]{:T(128)} %bitcast.121), kind=kOutput, calls=%fused_computation.36 | convolution fusion | flops 11477120 | bytes 399556 | tf_op jit(solution)/shard_map/jvp()/conv_general_dilated | solution.py:74
  300.2 2.1 copy.116
  303.6 2.7 fusion.226
  306.4 1.9 copy.124
  310.3 1.4 copy.142
  311.7 1.4 copy.143
  314.5 23.1 %fusion.238 = (f32[16]{0:T(128)S(1)}, f32[10,4,8,17,16]{4,2,3,1,0:T(8,128)}) fusion(f32[16]{0:T(128)S(1)} %copy-done.26, f32[10,4,8,17,16]{4,2,3,1,0:T(8,128)} %copy-done.5, f32[10,4]{1,0:T(8,128)S(1)} %broadcast_multiply_fusion.3, f32[1,16,3,3,3]{1,0,4,3,2:T(1,128)S(1)} %copy-done.28, pred[8,17]{0,1:T(8,128)(4,1)S(1)} %copy-done.22, ...), kind=kOutput, calls=%fused_computation.377 | convolution fusion | flops 12150768 | bytes 708200 | tf_op jit(solution)/shard_map/transpose(jvp())/conv_general_dilated | solution.py:74
  337.9 2.5 maximum_bitcast_fusion.2
  340.4 1.5 fusion.25
  342.5 53.9 %fusion.31 = f32[16,2,3,3,3]{0,1,4,3,2:T(2,128)S(1)} fusion(f32[10,4,8,17,16]{4,2,3,1,0:T(8,128)S(1)} %copy-done.29, f32[2,12,6,8,17,1]{3,0,5,4,2,1:T(2,128)S(1)} %get-tuple-element.82, f32[2,12,6,8,17,1]{3,0,5,4,2,1:T(2,128)S(1)} %copy-done.10, f32[2,12,6,8,17,1]{3,0,5,4,2,1:T(2,128)S(1)} %get-tuple-element.81), kind=kOutput, calls=%fused_computation.52 | convolution fusion | flops 56519424 | bytes 586624 | tf_op jit(solution)/shard_map/transpose(jvp())/conv_general_dilated | solution.py:74
  396.4 13.1 %fusion.36 = f32[1,16,3,3,3]{1,0,4,3,2:T(1,128)S(1)} fusion(f32[1,8,2,8,17,1]{3,0,5,4,2,1:T(1,128)S(1)} %copy.130, f32[10,4,8,17,16,1]{4,2,3,1,0,5:T(8,128)S(1)} %get-tuple-element.84, f32[10,4,8,17,16,1]{4,2,3,1,0,5:T(8,128)S(1)} %copy-done.4, f32[10,4,8,17,16,1]{4,2,3,1,0,5:T(8,128)S(1)} %get-tuple-element.83), kind=kOutput, calls=%fused_computation.53 | convolution fusion | flops 11802624 | bytes 1054912 | tf_op jit(solution)/shard_map/transpose(jvp())/conv_general_dilated | solution.py:74
  409.5 103.5 %all-reduce.4 = (f32[16,2,3,3,3]{0,1,4,3,2:T(2,128)S(1)}, f32[16]{0:T(128)S(1)}, f32[1,16,3,3,3]{1,0,4,3,2:T(1,128)S(1)}, f32[1]{0:T(128)}) all-reduce(f32[16,2,3,3,3]{0,1,4,3,2:T(2,128)S(1)} %fusion.31, f32[16]{0:T(128)S(1)} %get-tuple-element.79, ...), channel_id=1, replica_groups=mesh['shot'=32,'sub'=16] {'shot','sub'}, use_global_device_ids=true, to_apply=%region_1.2 | all-reduce | flops 1313 | bytes 10504 | tf_op jit(solution)/shard_map/psum | solution.py:176
  (136 shorter events, 26.3 us)
Async XLA Ops:
  7.2 206.9 %copy-start = (f32[16,2,3,3,3]{0,1,4,3,2:T(2,128)S(1)}, f32[16,2,3,3,3]{0,1,4,3,2:T(2,128)}, u32[]{:S(2)}) copy-start(f32[16,2,3,3,3]{0,1,4,3,2:T(2,128)} %param.24) | copy-start | bytes 10372
  7.2 7.2 %copy-start.11 = (bf16[1,8,64,128]{3,2,1,0:T(8,128)(2,1)S(1)}, bf16[1,8,64,128]{3,2,1,0:T(8,128)(2,1)}, u32[]{:S(2)}) copy-start(bf16[1,8,64,128]{3,2,1,0:T(8,128)(2,1)} %param.15) | copy-start | bytes 393220
  7.2 12.2 %copy-start.25 = (f32[1,2]{1,0:T(1,128)S(1)}, f32[1,2]{1,0:T(1,128)}, u32[]{:S(2)}) copy-start(f32[1,2]{1,0:T(1,128)} %param.21) | copy-start | bytes 28
  7.2 12.7 %copy-start.21 = (s32[1,3]{1,0:T(1,128)S(1)}, s32[1,3]{1,0:T(1,128)}, u32[]{:S(2)}) copy-start(s32[1,3]{1,0:T(1,128)} %param.20) | copy-start | bytes 40
  7.2 14.6 %copy-start.23 = (s32[1,256,2]{1,2,0:T(2,128)S(1)}, s32[1,256,2]{1,2,0:T(2,128)}, u32[]{:S(2)}) copy-start(s32[1,256,2]{1,2,0:T(2,128)} %param.22) | copy-start | bytes 6148
  7.2 14.6 %copy-start.24 = (f32[1,2,256]{2,1,0:T(2,128)S(1)}, f32[1,2,256]{2,1,0:T(2,128)}, u32[]{:S(2)}) copy-start(f32[1,2,256]{2,1,0:T(2,128)} %param.23) | copy-start | bytes 6148
  7.2 14.7 %copy-start.19 = (f32[8,2,128]{2,1,0:T(2,128)S(1)}, f32[8,2,128]{2,1,0:T(2,128)}, u32[]{:S(2)}) copy-start(f32[8,2,128]{2,1,0:T(2,128)} %param.18) | copy-start | bytes 24580
  7.2 185.4 %reduce-scatter.2.cloned.1.call-start = ((), (), s32[]{:S(2)}) async-start(), calls=%async_computation.1 | async-start | bytes 270336 | tf_op jit(solution)/shard_map/reduce_scatter | solution.py:149
  8.4 75.2 %collective-permute-start.4 = (f32[4,64,128]{2,0,1:T(4,128)S(1)}, f32[4,64,128]{2,0,1:T(4,128)S(1)}, u32[]{:S(2)}, u32[]{:S(2)}) collective-permute-start(f32[4,64,128]{2,0,1:T(4,128)S(1)} %get-tuple-element.54), channel_id=1, source_target_pairs={{1,0},{2,1},{3,2},{4,3},{5,4},{6,5},{7,6},{8,7},{9,8},{10,9},{11,1... | collective-permute-start | bytes 393224 | tf_op jit(solution)/shard_map/ppermute | solution.py:26
  9.7 73.9 %collective-permute-start.5 = (f32[4,64,128]{2,0,1:T(4,128)S(1)}, f32[4,64,128]{2,0,1:T(4,128)S(1)}, u32[]{:S(2)}, u32[]{:S(2)}) collective-permute-start(f32[4,64,128]{2,0,1:T(4,128)S(1)} %get-tuple-element.55), channel_id=1, source_target_pairs={{0,1},{1,2},{2,3},{3,4},{4,5},{5,6},{6,7},{7,8},{8,9},{9,10},{10,1... | collective-permute-start | bytes 393224 | tf_op jit(solution)/shard_map/ppermute | solution.py:24
  14.5 61.5 %copy-start.17 = (bf16[1,8,64,128]{3,2,1,0:T(8,128)(2,1)S(1)}, bf16[1,8,64,128]{3,2,1,0:T(8,128)(2,1)}, u32[]{:S(2)}) copy-start(bf16[1,8,64,128]{3,2,1,0:T(8,128)(2,1)} %param.14) | copy-start | bytes 393220
  14.5 60.9 %collective-permute-start.1 = (f32[4,64,128]{2,0,1:T(4,128)S(1)}, f32[4,64,128]{2,0,1:T(4,128)S(1)}, u32[]{:S(2)}, u32[]{:S(2)}) collective-permute-start(f32[4,64,128]{2,0,1:T(4,128)S(1)} %get-tuple-element.56), channel_id=1, source_target_pairs={{0,1},{1,2},{2,3},{3,4},{4,5},{5,6},{6,7},{7,8},{8,9},{9,10},{10,1... | collective-permute-start | bytes 393224 | tf_op jit(solution)/shard_map/ppermute | solution.py:24
  18.0 57.4 %collective-permute-start = (f32[4,64,128]{2,0,1:T(4,128)S(1)}, f32[4,64,128]{2,0,1:T(4,128)S(1)}, u32[]{:S(2)}, u32[]{:S(2)}) collective-permute-start(f32[4,64,128]{2,0,1:T(4,128)S(1)} %get-tuple-element.57), channel_id=1, source_target_pairs={{1,0},{2,1},{3,2},{4,3},{5,4},{6,5},{7,6},{8,7},{9,8},{10,9},{11,1... | collective-permute-start | bytes 393224 | tf_op jit(solution)/shard_map/ppermute | solution.py:26
  77.9 6.3 %copy-start.18 = (bf16[1,8,64,128]{3,2,1,0:T(8,128)(2,1)S(1)}, bf16[1,8,64,128]{3,2,1,0:T(8,128)(2,1)}, u32[]{:S(2)}) copy-start(bf16[1,8,64,128]{3,2,1,0:T(8,128)(2,1)} %param.16) | copy-start | bytes 393220
  77.9 14.1 %collective-permute-start.3 = (f32[4,64,128]{2,0,1:T(4,128)S(1)}, f32[4,64,128]{2,0,1:T(4,128)S(1)}, u32[]{:S(2)}, u32[]{:S(2)}) collective-permute-start(f32[4,64,128]{2,0,1:T(4,128)S(1)} %get-tuple-element.50), channel_id=1, source_target_pairs={{0,1},{1,2},{2,3},{3,4},{4,5},{5,6},{6,7},{7,8},{8,9},{9,10},{10,1... | collective-permute-start | bytes 393224 | tf_op jit(solution)/shard_map/ppermute | solution.py:24
  82.3 9.7 %collective-permute-start.2 = (f32[4,64,128]{2,0,1:T(4,128)S(1)}, f32[4,64,128]{2,0,1:T(4,128)S(1)}, u32[]{:S(2)}, u32[]{:S(2)}) collective-permute-start(f32[4,64,128]{2,0,1:T(4,128)S(1)} %get-tuple-element.51), channel_id=1, source_target_pairs={{1,0},{2,1},{3,2},{4,3},{5,4},{6,5},{7,6},{8,7},{9,8},{10,9},{11,1... | collective-permute-start | bytes 393224 | tf_op jit(solution)/shard_map/ppermute | solution.py:26
  85.4 8.1 %collective-permute-start.6 = (f32[4,64,128]{2,0,1:T(4,128)S(1)}, f32[4,64,128]{2,0,1:T(4,128)S(1)}, u32[]{:S(2)}, u32[]{:S(2)}) collective-permute-start(f32[4,64,128]{2,0,1:T(4,128)S(1)} %get-tuple-element.52), channel_id=1, source_target_pairs={{1,0},{2,1},{3,2},{4,3},{5,4},{6,5},{7,6},{8,7},{9,8},{10,9},{11,1... | collective-permute-start | bytes 393224 | tf_op jit(solution)/shard_map/ppermute | solution.py:26
  86.7 7.6 %collective-permute-start.7 = (f32[4,64,128]{2,0,1:T(4,128)S(1)}, f32[4,64,128]{2,0,1:T(4,128)S(1)}, u32[]{:S(2)}, u32[]{:S(2)}) collective-permute-start(f32[4,64,128]{2,0,1:T(4,128)S(1)} %get-tuple-element.53), channel_id=1, source_target_pairs={{0,1},{1,2},{2,3},{3,4},{4,5},{5,6},{6,7},{7,8},{8,9},{9,10},{10,1... | collective-permute-start | bytes 393224 | tf_op jit(solution)/shard_map/ppermute | solution.py:24
  193.3 7.7 %collective-permute-start.9 = (f32[2,8,2,128]{3,1,2,0:T(8,128)S(1)}, f32[2,8,2,128]{3,1,2,0:T(8,128)S(1)}, u32[]{:S(2)}, u32[]{:S(2)}) collective-permute-start(f32[2,8,2,128]{3,1,2,0:T(8,128)S(1)} %pad_maximum_fusion.9), channel_id=1, source_target_pairs={{16,0},{32,16},{48,32},{64,48},{80,64},{96,80},{112,96},{128,112},... | collective-permute-start | bytes 49160 | tf_op jit(solution)/shard_map/ppermute | solution.py:26
  197.8 3.3 collective-permute-start.8
  201.1 5.9 %collective-permute-start.10 = (f32[2,2,6,128]{3,1,2,0:T(2,128)S(1)}, f32[2,2,6,128]{3,1,2,0:T(2,128)S(1)}, u32[]{:S(2)}, u32[]{:S(2)}) collective-permute-start(f32[2,2,6,128]{3,1,2,0:T(2,128)S(1)} %get-tuple-element.64), channel_id=1, source_target_pairs={{0,1},{1,2},{2,3},{3,4},{4,5},{5,6},{6,7},{7,8},{8,9},{9,10},{10,1... | collective-permute-start | bytes 36872 | tf_op jit(solution)/shard_map/ppermute | solution.py:24
  204.2 4.4 collective-permute-start.11
  214.1 31.9 %copy-start.22 = (pred[8,17]{0,1:T(8,128)(4,1)S(1)}, pred[8,17]{0,1:T(8,128)(4,1)}, u32[]{:S(2)}) copy-start(pred[8,17]{0,1:T(8,128)(4,1)} %constant.100) | copy-start | bytes 412
  214.1 31.9 %copy-start.26 = (f32[16]{0:T(128)S(1)}, f32[16]{0:T(128)}, u32[]{:S(2)}) copy-start(f32[16]{0:T(128)} %param.25) | copy-start | bytes 196
  306.4 2.9 copy-start.8
  306.4 3.9 copy-start.7
  311.7 2.7 copy-start.28
  314.5 23.3 %copy-start.1 = (f32[10,4,1,8,16,16]{5,3,4,1,0,2:T(8,128)S(1)}, f32[10,4,1,8,16,16]{5,3,4,1,0,2:T(8,128)}, u32[]{:S(2)}) copy-start(f32[10,4,1,8,16,16]{5,3,4,1,0,2:T(8,128)} %get-tuple-element.42) | copy-start | bytes 983044
  314.5 23.3 %copy-start.13 = (f32[10,4,1,8,1,16]{5,3,4,1,0,2:T(8,128)S(1)}, f32[10,4,1,8,1,16]{5,3,4,1,0,2:T(8,128)}, u32[]{:S(2)}) copy-start(f32[10,4,1,8,1,16]{5,3,4,1,0,2:T(8,128)} %copy-done.12) | copy-start | bytes 61444
  314.5 23.3 %copy-start.15 = (f32[10,4,1,8,1,16]{5,3,4,1,0,2:T(8,128)S(1)}, f32[10,4,1,8,1,16]{5,3,4,1,0,2:T(8,128)}, u32[]{:S(2)}) copy-start(f32[10,4,1,8,1,16]{5,3,4,1,0,2:T(8,128)} %copy-done.14) | copy-start | bytes 61444
  337.8 2.5 copy-start.2
  342.5 53.9 %copy-start.4 = (f32[10,4,8,17,16,1]{4,2,3,1,0,5:T(8,128)S(1)}, f32[10,4,8,17,16,1]{4,2,3,1,0,5:T(8,128)}, u32[]{:S(2)}) copy-start(f32[10,4,8,17,16,1]{4,2,3,1,0,5:T(8,128)} %get-tuple-element.40) | copy-start | bytes 1044484
  (11 other events, 19.7 us)
Sparse Core Ops, SparseCore 0:
  98.4 94.1 reduce-scatter.1
where the time goes:
time: 538 us; the launch traced here: 529 us
  matrix products  174 us (32%)
  blocking collectives  156 us (29%)
  waiting for transfers between devices  97.8 us (18%)
  starting transfers between devices  34.2 us (6%)
  other arithmetic  24.9 us (5%)
  between operations  21.6 us (4%)
  local copies, waits for them, and re-layouts  21.1 us (4%)
    conv_general_dilated x5, matrix products, convolve(): lax.conv_general_dilated(inputs, kernel, (1, 1, 1), pads, dimension_numbe...  173 us
    psum x1, blocking collectives, shards(): lax.psum((local_terms[0], local_terms[1], local_terms[2], local_terms[3])...  104 us
    reduce_scatter x1, waiting for transfers between devices, shards(): lax.psum_scatter(image_term, 'shot', scatter_dimension=1, tiled=True)  94.3 us
    all_gather x1, blocking collectives, shards(): model_full = lax.all_gather(velocity, 'shot', axis=1, tiled=True)  52.1 us
    ppermute x6, starting transfers between devices, extended_2(): lax.ppermute(tail, axis, [(i, (i + 1) % count) for i in range(ends)])  23.2 us
    ppermute x6, starting transfers between devices, extended_2(): lax.ppermute(head, axis, [((i + 1) % count, i) for i in range(ends)])  11 us
  transfers between devices with their start and end apart: 13, of which 5 were waited for; matrix products, arithmetic and copies ran while one was open for 2% of the time, Pallas kernels for 0%

commit v1 on v0

v1 whole, which is shorter than its diff:
```python
import functools

import jax
import jax.numpy as jnp
from jax import lax
from jax.experimental import pallas as pl
from jax.experimental.pallas import tpu as pltpu
from jax.sharding import PartitionSpec as P

F32 = jnp.float32
BF16 = jnp.bfloat16
MESH = pl.DeviceIdType.MESH

ZREC = 2
COEFFS = (-205.0 / 72.0, 8.0 / 5.0, -1.0 / 5.0, 8.0 / 315.0, -1.0 / 560.0)
CENTER_SHIFT = 0.125
CENTER_GAIN = 16.0
ENTRIES = 1313

ROWS = 8
COLS = 64
DEPTH = 128
PAD = 8
N_SHOT, N_SUB = 32, 16
GRID_X, GRID_Y = 128, 64

TILES = 80
WIDE = 12
HID = 48 * DEPTH
CHUNK = 8 * DEPTH
OFFSETS = tuple(dy * WIDE + dx for dx in range(3) for dy in range(3))
BLOCKS = 10


def dot(a, b):
    return jnp.dot(a, b, preferred_element_type=F32)


def dot_t(a, b):
    return lax.dot_general(a, b, (((1,), (1,)), ((), ())), preferred_element_type=F32)


def halves(x):
    high = x.astype(BF16)
    return high, (x - high.astype(F32)).astype(BF16)


def shifted(x, dz):
    if dz == 0:
        return x
    z = lax.broadcasted_iota(jnp.int32, x.shape, 1)
    if dz > 0:
        return jnp.where(z < DEPTH - dz, pltpu.roll(x, DEPTH - dz, 1), 0.0)
    return jnp.where(z >= -dz, pltpu.roll(x, -dz, 1), 0.0)


def kernel(
    wb, wn, ab, an, vel, tgt, scell, swave, rcell, rtrace, wpack, b2,
    nw, nv, moves,
    p0, q0, p1, q1, lap0, imgacc, vfull, vg, surf, imgt, ra, acca, rb, hb_img, hb_vel,
    ext, gs, g2, rs, r2, fhi, flo, hid, smat, tt, mask, re,
    s_hal, r_hal, s_v1, r_v1, s_v2, r_v2, s_hv, r_hv, s_a, r_a, s_b, r_b, s_c, r_c, s_e, r_e,
):
    shot = lax.axis_index("shot")
    sub = lax.axis_index("sub")
    zh, xc = shot // 8, shot % 8
    zlo, yy = sub // 8, sub % 8
    zz = zh * 2 + zlo
    x0 = sub * ROWS
    up, down = (sub + 1) % N_SUB, (sub + N_SUB - 1) % N_SUB

    def xc_peer(k):
        return (zh * 8 + (xc + k) % 8, sub)

    def zh_peer(k):
        return (((zh + k) % 4) * 8 + xc, sub)

    def z_peer(k):
        z = (zz + k) % 8
        return ((z // 2) * 8 + xc, (z % 2) * 8 + yy)

    def y_peer(k):
        return (shot, zlo * 8 + (yy + k) % 8)

    def near(d, e):
        return ((shot + d + N_SHOT) % N_SHOT, (sub + e + N_SUB) % N_SUB)

    around = [(d, e) for d in (-1, 0, 1) for e in (-1, 0, 1) if (d, e) != (0, 0)]
    greeted = (
        [near(d, e) for d, e in around]
        + [xc_peer(k) for k in range(1, 8)]
        + [zh_peer(k) for k in range(1, 4)]
        + [z_peer(k) for k in range(1, 8)]
        + [y_peer(k) for k in range(1, 8)]
    )
    barrier = pltpu.get_barrier_semaphore()
    for device in greeted:
        pl.semaphore_signal(barrier, inc=1, device_id=device, device_id_type=MESH)

    pending = []

    def send(src, dst, ssem, rsem, device):
        copy = pltpu.make_async_remote_copy(
            src_ref=src, dst_ref=dst, send_sem=ssem, recv_sem=rsem, device_id=device, device_id_type=MESH
        )
        copy.start()
        pending.append(copy)
        return copy

    zeros_pad = jnp.zeros((16, PAD, DEPTH), F32)
    for field in (p0, q0, p1, q1):
        field[:, 0:PAD, :] = zeros_pad
        field[:, PAD + COLS :, :] = zeros_pad
    p0[4:12, PAD : PAD + COLS, :] = wn[0].astype(F32)
    q0[4:12, PAD : PAD + COLS, :] = an[0].astype(F32)
    for j in range(2):
        hb_vel[4, j * 8 : (j + 1) * 8, :] = vel[:, j, :]
    own = pl.ds(pl.multiple_of(xc * 16, 16), 16)
    vg[zh, own, :] = hb_vel[4]

    pl.semaphore_wait(barrier, len(greeted))

    def halo(field, index):
        inner = pl.ds(PAD, COLS)
        a = send(
            field.at[pl.ds(8, 4), inner, :], field.at[pl.ds(0, 4), inner, :],
            s_hal.at[index], r_hal.at[index], (shot, up),
        )
        b = send(
            field.at[pl.ds(4, 4), inner, :], field.at[pl.ds(12, 4), inner, :],
            s_hal.at[index + 1], r_hal.at[index + 1], (shot, down),
        )
        return a, b

    def halo_wait(field, copies):
        for copy in copies:
            copy.wait_recv()

        @pl.when(sub == 0)
        def _():
            field[0:4, PAD : PAD + COLS, :] = jnp.zeros((4, COLS, DEPTH), F32)

        @pl.when(sub == N_SUB - 1)
        def _():
            field[12:16, PAD : PAD + COLS, :] = jnp.zeros((4, COLS, DEPTH), F32)

    v1 = [
        send(hb_vel.at[4], vg.at[zh, own, :], s_v1.at[k - 1], r_v1.at[k - 1], zh_peer(k)) for k in range(1, 4)
    ]
    halo_p0 = halo(p0, 0)
    halo_q0 = halo(q0, 2)
    for copy in v1:
        copy.wait_recv()
    v2 = [
        send(vg.at[:, own, :], vg.at[:, own, :], s_v2.at[k - 1], r_v2.at[k - 1], xc_peer(k)) for k in range(1, 8)
    ]

    def around_sends(buffer, ssem, rsem):
        return [
            send(
                buffer.at[4], buffer.at[(1 - d) * 3 + (1 - e)], ssem.at[n], rsem.at[n], near(d, e)
            )
            for n, (d, e) in enumerate(around)
        ]

    hv = around_sends(hb_vel, s_hv, r_hv)

    cells = rcell[0].astype(F32).astype(BF16)
    pick = (
        lax.broadcasted_iota(jnp.int32, (8, 2), 0) == lax.broadcasted_iota(jnp.int32, (8, 2), 1)
    ).astype(F32).astype(BF16)
    cells_t = dot_t(pick, cells)
    rec_x = cells_t[0:1, :]
    rec_y = cells_t[1:2, :]
    hit_y = (
        lax.broadcasted_iota(jnp.int32, (COLS, 256), 0).astype(F32) == jnp.broadcast_to(rec_y, (COLS, 256))
    ).astype(F32).astype(BF16)
    rows_here = (lax.broadcasted_iota(jnp.int32, (8, 256), 0) + x0).astype(F32)
    hit_x = (rows_here == jnp.broadcast_to(rec_x, (8, 256))).astype(F32)
    trace = jnp.concatenate([hit_x * rtrace[0, 0:1, :], hit_x * rtrace[0, 1:2, :]], axis=0)
    t_hi, t_rest = trace.astype(BF16), trace - trace.astype(BF16).astype(F32)
    t_mid, t_lo = halves(t_rest)
    surf[:, 0:16] = dot_t(hit_y, t_hi) + dot_t(hit_y, t_mid) + dot_t(hit_y, t_lo)

    lane = lax.broadcasted_iota(jnp.int32, (16, HID), 1)
    tile = lane >> 7
    hid_y = (tile >= 12).astype(jnp.int32) + (tile >= 24).astype(jnp.int32) + (tile >= 36).astype(jnp.int32)
    hid_x = tile - 12 * hid_y
    cell_x = hid_x + (x0 - 1)
    cell_y = hid_y + (2 * shot - 1)
    mask[...] = (
        (hid_x < 10) & (cell_x >= 0) & (cell_x < GRID_X) & (cell_y >= 0) & (cell_y < GRID_Y)
    ).astype(F32)
    gs[...] = jnp.where(lax.broadcasted_iota(jnp.int32, (TILES * 8, DEPTH), 0) % 8 == 6, 1.0, 0.0)
    rs[...] = jnp.zeros((TILES * 8, DEPTH), F32)

    z_row = lax.broadcasted_iota(jnp.int32, (COLS, DEPTH), 1)
    y_row = lax.broadcasted_iota(jnp.int32, (COLS, DEPTH), 0)
    source_yz = jnp.where((y_row == scell[0, 1]) & (z_row == scell[0, 2]), 1.0, 0.0)
    rec_mark = z_row == ZREC
    back_w = [None] + [jnp.where(z_row[0:8] >= k, COEFFS[k], 0.0) for k in range(1, 5)]
    fore_w = [None] + [jnp.where(z_row[0:8] < DEPTH - k, COEFFS[k], 0.0) for k in range(1, 5)]

    def tall(w):
        return jnp.broadcast_to(w[0:1], (COLS, DEPTH))

    def lap_row(field, i):
        inner = pl.ds(PAD, COLS)
        center = field[i + 4, inner, :]
        out = (3.0 * COEFFS[0]) * center
        for k in range(1, 5):
            out = out + COEFFS[k] * (
                (field[i + 4 + k, inner, :] + field[i + 4 - k, inner, :])
                + (field[i + 4, pl.ds(PAD + k, COLS), :] + field[i + 4, pl.ds(PAD - k, COLS), :])
            )
            out = out + pltpu.roll(center, k, 1) * tall(back_w[k])
            out = out + pltpu.roll(center, DEPTH - k, 1) * tall(fore_w[k])
        return center, out

    def source(i, step):
        amount = jnp.where(scell[0, 0] == x0 + i, swave[0, step], 0.0)
        return amount * source_yz

    def receivers(i, step):
        column = pltpu.roll(surf[...], (DEPTH + ZREC - step * 8 - i) % DEPTH, 1)
        return jnp.where(rec_mark, column, 0.0)

    for copy in v2:
        copy.wait_recv()
    for z in range(4):
        for i in range(ROWS):
            vfull[i, z * 16 : (z + 1) * 16, :] = vg.at[z][pl.ds(i, 16, stride=8), :]
    halo_wait(p0, halo_p0)

    def forward_0(i, carry):
        center, lap = lap_row(p0, i)
        lap0[i] = lap
        p1[i + 4, pl.ds(PAD, COLS), :] = (
            2.0 * center - wb[0, i].astype(F32) + vfull[i] * lap + source(i, 0)
        )
        return carry

    lax.fori_loop(0, ROWS, forward_0, 0)
    halo_p1 = halo(p1, 4)

    halo_wait(q0, halo_q0)

    def adjoint_0(i, carry):
        center, lap = lap_row(q0, i)
        q1[i + 4, pl.ds(PAD, COLS), :] = (
            2.0 * center - ab[0, i].astype(F32) + vfull[i] * lap + receivers(i, 0)
        )
        return carry

    lax.fori_loop(0, ROWS, adjoint_0, 0)
    halo_q1 = halo(q1, 6)

    ok_shot = {-1: shot > 0, 0: None, 1: shot < N_SHOT - 1}
    ok_sub = {-1: sub > 0, 0: None, 1: sub < N_SUB - 1}

    def channel(buffer, which, centered):
        for d in (-1, 0, 1):
            for e in (-1, 0, 1):
                for j in range(2):
                    block = buffer[(d + 1) * 3 + (e + 1), j * 8 : (j + 1) * 8, :]
                    if centered:
                        block = (block - CENTER_SHIFT) * CENTER_GAIN
                    for ok in (ok_shot[d], ok_sub[e]):
                        if ok is not None:
                            block = block * jnp.where(ok, 1.0, 0.0)
                    row = (2 + 2 * d + j) * WIDE
                    if e == -1:
                        ext[row : row + 2, :] = block[6:8]
                    elif e == 0:
                        ext[row + 2 : row + 10, :] = block
                    else:
                        ext[row + 10 : row + 12, :] = block[0:2]
        value = ext[...]
        for dz in range(3):
            gs[pl.ds(which * 3 + dz, 72, stride=8), :] = shifted(value, dz - 1)

    for copy in hv:
        copy.wait_recv()
    channel(hb_vel, 1, True)

    halo_wait(p1, halo_p1)

    def forward_1(i, carry):
        center, lap = lap_row(p1, i)
        fresh = 2.0 * center - p0[i + 4, pl.ds(PAD, COLS), :] + vfull[i] * lap + source(i, 1)
        nw[0, i] = fresh.astype(BF16)
        imgacc[i] = lap * q1[i + 4, pl.ds(PAD, COLS), :]
        return carry

    lax.fori_loop(0, ROWS, forward_1, 0)

    halo_wait(q1, halo_q1)

    def adjoint_1(i, carry):
        center, lap = lap_row(q1, i)
        fresh = 2.0 * center - q0[i + 4, pl.ds(PAD, COLS), :] + vfull[i] * lap + receivers(i, 1)
        imgacc[i] = imgacc[i] + lap0[i] * fresh
        return carry

    lax.fori_loop(0, ROWS, adjoint_1, 0)
    for z in range(4):
        for i in range(ROWS):
            imgt.at[z][pl.ds(i, 16, stride=8), :] = imgacc[i, z * 16 : (z + 1) * 16, :]

    sends_a = [
        send(
            imgt.at[:, pl.ds(pl.multiple_of(((xc + k) % 8) * 16, 16), 16), :], ra.at[k - 1],
            s_a.at[k - 1], r_a.at[k - 1], xc_peer(k),
        )
        for k in range(1, 8)
    ]
    total = imgt[:, own, :]
    for k in range(1, 8):
        sends_a[k - 1].wait_recv()
        total = total + ra[k - 1]
    acca[...] = total
    sends_b = [
        send(acca.at[(zh + k) % 4], rb.at[k - 1], s_b.at[k - 1], r_b.at[k - 1], zh_peer(k)) for k in range(1, 4)
    ]
    total = acca[zh]
    for k in range(1, 4):
        sends_b[k - 1].wait_recv()
        total = total + rb[k - 1]
    hb_img[4] = total * (1.0 / N_SHOT)
    sends_c = around_sends(hb_img, s_c, r_c)

    w1, k2 = wpack[:, 0:80], wpack[:, 128:208]
    w1_hi, w1_lo = halves(w1)
    k2_hi, k2_lo = halves(k2)
    w1_cat = jnp.concatenate([w1_hi, w1_hi, w1_lo], axis=1)
    k2_cat = jnp.concatenate([k2_hi, k2_hi, k2_lo], axis=1)
    unit = (
        lax.broadcasted_iota(jnp.int32, (80, 80), 0) == lax.broadcasted_iota(jnp.int32, (80, 80), 1)
    ).astype(F32).astype(BF16)
    k2t_hi = dot_t(unit, k2_hi).astype(BF16)
    k2t_lo = dot_t(unit, k2_lo).astype(BF16)
    k2t_cat = jnp.concatenate([k2t_hi, k2t_hi, k2t_lo], axis=1)

    for copy in sends_c:
        copy.wait_recv()
    channel(hb_img, 0, False)

    def spread(source_ref, target_ref):
        for t in range(TILES):
            target_ref[:, t * DEPTH : (t + 1) * DEPTH] = source_ref[t * 8 : (t + 1) * 8, :]

    def stacked(ref, offsets, start):
        parts = [ref[:, start + o * DEPTH : start + o * DEPTH + CHUNK] for o in offsets]
        return jnp.concatenate(parts, axis=0)

    spread(gs, g2)
    for start in range(0, HID, CHUNK):
        here = slice(start, start + CHUNK)
        f_hi, f_lo = halves(stacked(g2, OFFSETS + (0,), start))
        fhi[:, here] = f_hi
        flo[:, here] = f_lo
        pre = dot(w1_cat, jnp.concatenate([f_hi, f_lo, f_hi], axis=0))
        hidden = jnp.tanh(pre) * mask[:, here]
        hid[:, here] = hidden
        h_hi, h_lo = halves(hidden)
        smat[:, here] = dot(k2t_cat, jnp.concatenate([h_hi, h_lo, h_hi], axis=0))

    span = 20 * DEPTH
    turned = smat[0:8, 0:span]
    for n in range(1, 9):
        turned = turned + smat[n * 8 : n * 8 + 8, OFFSETS[n] * DEPTH : OFFSETS[n] * DEPTH + span]
    for t in range(20):
        tt[t * 8 : t * 8 + 8, :] = turned[:, t * DEPTH : (t + 1) * DEPTH]
    bias_sum = jnp.zeros((8, DEPTH), F32)
    for j in range(2):
        update = b2[0]
        for dz in range(3):
            update = update + shifted(tt[pl.ds(j * WIDE * 8 + dz, 8, stride=8), :], dz - 1)
        fresh = hb_vel[4, j * 8 : (j + 1) * 8, :] - update
        nv[:, j, :] = fresh
        slope = tgt[:, j, :] - fresh
        bias_sum = bias_sum + slope
        for dz in range(3):
            rs[pl.ds(((j + 2) * WIDE + 2) * 8 + dz, 8, stride=8), :] = shifted(slope, 1 - dz)

    spread(rs, r2)
    offsets_r = tuple((2 - dy) * WIDE + (2 - dx) for dx in range(3) for dy in range(3)) + (0,)
    grad_1 = jnp.zeros((32, 160), F32)
    grad_2 = jnp.zeros((32, 160), F32)
    for start in range(0, HID, CHUNK):
        here = slice(start, start + CHUNK)
        r_hi, r_lo = halves(stacked(r2, offsets_r, start))
        slope_h = dot(k2_cat, jnp.concatenate([r_hi, r_lo, r_hi], axis=0))
        hidden = hid[:, here]
        h_hi, h_lo = halves(hidden)
        grad_2 = grad_2 + dot_t(jnp.concatenate([h_hi, h_lo], axis=0), jnp.concatenate([r_hi, r_lo], axis=0))
        d_hi, d_lo = halves(slope_h * (1.0 - hidden * hidden) * mask[:, here])
        grad_1 = grad_1 + dot_t(
            jnp.concatenate([d_hi, d_lo], axis=0), jnp.concatenate([fhi[:, here], flo[:, here]], axis=0)
        )

    def joined(grad):
        value = (grad[0:16, 0:80] + grad[0:16, 80:160]) + grad[16:32, 0:80]
        return jnp.concatenate([value, jnp.zeros((16, 48), F32)], axis=1)

    gk1, gk2 = joined(grad_1), joined(grad_2)
    col = lax.broadcasted_iota(jnp.int32, (16, DEPTH), 1)
    row = lax.broadcasted_iota(jnp.int32, (16, DEPTH), 0)
    pack = jnp.where((col < 72) & ((col % 8 < 6) | (col == 38)), gk1, 0.0)
    for n in range(9):
        moved = pltpu.roll(gk2, 72 + 3 * n - 8 * n, 1)
        pack = jnp.where((col >= 72 + 3 * n) & (col < 75 + 3 * n), moved, pack)
    bias = jnp.sum(jnp.sum(bias_sum, axis=0, keepdims=True), axis=1, keepdims=True)
    pack = jnp.where((col == 99) & (row == 0), jnp.broadcast_to(bias, (16, DEPTH)), pack)

    for level, (me, peer) in enumerate(((xc, xc_peer), (zz, z_peer), (yy, y_peer))):
        re[level, me] = pack
        copies = [
            send(
                re.at[level, me], re.at[level, me], s_e.at[level * 7 + k - 1], r_e.at[level * 7 + k - 1], peer(k)
            )
            for k in range(1, 8)
        ]
        for copy in copies:
            copy.wait_recv()
        pack = re[level, 0]
        for n in range(1, 8):
            pack = pack + re[level, n]

    squares = jnp.sum(jnp.sum(pack * pack, axis=0, keepdims=True), axis=1, keepdims=True)
    factor = 1.0 / jnp.sqrt(squares * (1.0 / ENTRIES) + 1e-06)
    moves[...] = pack * factor

    for copy in pending:
        copy.wait_send()


def shards(
    wave_before, wave_now, adjoint_before, adjoint_now, velocity, target_model, source_cell, source_wave,
    receiver_cell, receiver_trace, first_kernel, first_bias, second_kernel, second_bias,
):
    w1 = first_kernel.transpose(0, 2, 3, 1, 4).reshape(16, 9, 6)
    bias = jnp.zeros((16, 9, 1), F32).at[:, 4, 0].set(first_bias)
    w1 = jnp.pad(jnp.concatenate([w1, bias], axis=2), ((0, 0), (0, 0), (0, 1))).reshape(16, 72)
    k2 = jnp.pad(second_kernel.reshape(16, 9, 3), ((0, 0), (0, 0), (0, 5))).reshape(16, 72)
    wpack = jnp.concatenate([jnp.pad(w1, ((0, 0), (0, 56))), jnp.pad(k2, ((0, 0), (0, 56)))], axis=1)

    vmem = pl.BlockSpec(memory_space=pltpu.VMEM)
    smem = pl.BlockSpec(memory_space=pltpu.SMEM)
    dma = pltpu.SemaphoreType.DMA
    field = pltpu.VMEM((16, COLS + 2 * PAD, DEPTH), F32)
    block = pltpu.VMEM((ROWS, COLS, DEPTH), F32)
    scratch = [
        field, field, field, field, block, block, block,
        pltpu.VMEM((4, DEPTH, DEPTH), F32),
        pltpu.VMEM((COLS, DEPTH), F32),
        pltpu.VMEM((4, DEPTH, DEPTH), F32),
        pltpu.VMEM((7, 4, 16, DEPTH), F32),
        pltpu.VMEM((4, 16, DEPTH), F32),
        pltpu.VMEM((3, 16, DEPTH), F32),
        pltpu.VMEM((9, 16, DEPTH), F32),
        pltpu.VMEM((9, 16, DEPTH), F32),
        pltpu.VMEM((72, DEPTH), F32),
        pltpu.VMEM((TILES * 8, DEPTH), F32),
        pltpu.VMEM((8, TILES * DEPTH), F32),
        pltpu.VMEM((TILES * 8, DEPTH), F32),
        pltpu.VMEM((8, TILES * DEPTH), F32),
        pltpu.VMEM((80, HID), BF16),
        pltpu.VMEM((80, HID), BF16),
        pltpu.VMEM((16, HID), F32),
        pltpu.VMEM((80, HID), F32),
        pltpu.VMEM((160, DEPTH), F32),
        pltpu.VMEM((16, HID), F32),
        pltpu.VMEM((3, 8, 16, DEPTH), F32),
    ]
    for count in (8, 3, 7, 8, 7, 3, 8, 21):
        scratch += [dma((count,)), dma((count,))]
    next_wave, new_velocity, moves = pl.pallas_call(
        kernel,
        out_shape=(
            jax.ShapeDtypeStruct(wave_now.shape, BF16),
            jax.ShapeDtypeStruct(velocity.shape, F32),
            jax.ShapeDtypeStruct((16, DEPTH), F32),
        ),
        in_specs=[vmem, vmem, vmem, vmem, vmem, vmem, smem, smem, vmem, vmem, vmem, smem],
        out_specs=(vmem, vmem, vmem),
        scratch_shapes=scratch,
        compiler_params=pltpu.CompilerParams(
            collective_id=0, has_side_effects=True, vmem_limit_bytes=40 * 1024 * 1024
        ),
    )(
        wave_before, wave_now, adjoint_before, adjoint_now, velocity, target_model, source_cell, source_wave,
        receiver_cell, receiver_trace, wpack, second_bias,
    )
    taps = moves[:, 0:72].reshape(16, 3, 3, 8)
    first_move = taps[..., 0:6].reshape(16, 3, 3, 2, 3).transpose(0, 3, 1, 2, 4)
    return (
        next_wave,
        new_velocity,
        first_move,
        moves[:, 38],
        moves[:, 72:99].reshape(1, 16, 3, 3, 3),
        moves[0, 99:100],
    )


def solution(mesh):
    return jax.shard_map(
        shards,
        mesh=mesh,
        in_specs=(
            P("shot", "sub", None, None),
            P("shot", "sub", None, None),
            P("shot", "sub", None, None),
            P("shot", "sub", None, None),
            P("sub", "shot", None),
            P("sub", "shot", None),
            P("shot", None),
            P("shot", None),
            P("shot", None, None),
            P("shot", None, None),
            P(),
            P(),
            P(),
            P(),
        ),
        out_specs=(P("shot", "sub", None, None), P("sub", "shot", None), P(), P(), P(), P()),
        check_vma=False,
    )
```

time: 538 us -> 79.8 us (0.15); the launches traced: 529 us -> 79.2 us
  matrix products: 174 us -> 0 us
  blocking collectives: 156 us -> 0 us
  waiting for transfers between devices: 97.8 us -> 0 us
  Pallas kernels: 0 us -> 70.8 us
  starting transfers between devices: 34.2 us -> 0 us
  other arithmetic: 24.9 us -> 0.02 us
  between operations: 21.6 us -> 1.44 us
  local copies, waits for them, and re-layouts: 21.1 us -> 7 us
    conv_general_dilated x5 -> x0, matrix products: 173 us -> none  [convolve(): lax.conv_general_dilated(inputs, kernel, (1, 1, 1), pads, dimension_numbe...]
    psum x1 -> x0, blocking collectives: 104 us -> none  [shards(): lax.psum((local_terms[0], local_terms[1], local_terms[2], local_terms[3])...]
    reduce_scatter x1 -> x0, waiting for transfers between devices: 94.3 us -> none  [shards(): lax.psum_scatter(image_term, 'shot', scatter_dimension=1, tiled=True)]
    pallas_call x0 -> x1, Pallas kernels: none -> 70.8 us  [shards(): pl.pallas_call(kernel, out_shape=(jax.ShapeDtypeStruct(wave_now.shape, BF...]
    all_gather x1 -> x0, blocking collectives: 52.1 us -> none  [shards(): model_full = lax.all_gather(velocity, 'shot', axis=1, tiled=True)]
    ppermute x12 -> x0, starting transfers between devices: 34.2 us -> none  [the longest x6 23.2 us: extended_2(): lax.ppermute(tail, axis, [(i, (i + 1) % count) for i in range(ends)])]
    mul x7 -> x0, other arithmetic: 6.73 us -> none  [the longest x2 4.84 us: network(): hidden = jnp.tanh(pre_act) * inside[None, None, :, :, None]]
    add x4 -> x0, other arithmetic: 6.27 us -> none  [the longest x1 3.27 us: shards(): image_term = image_term + lap_list[step] * adjoint_list[STEPS - 1 - step]]
  transfers between devices with their start and end apart: 13 -> 0, of which waited for: 5 -> 0; matrix products, arithmetic and copies ran while one was open for 2% -> 0% of each run, Pallas kernels for 0% -> 0%
where the time goes in v1:
time: 79.8 us; the launch traced here: 79.2 us
  Pallas kernels  70.8 us (89%)
  local copies, waits for them, and re-layouts  7 us (9%)
  between operations  1.44 us (2%)
    pallas_call x1, Pallas kernels, shards(): pl.pallas_call(kernel, out_shape=(jax.ShapeDtypeStruct(wave_now.shape, BF...  70.8 us
    unnamed x29, local copies, waits for them, and re-layouts  4.68 us

profile of v1, /device:TPU:1, one launch (start us, length us, event | category | flops | bytes accessed | tf_op | source)
XLA Modules:
  0.0 79.2 jit_solution(16345597294960696662)
XLA Ops:
  1.3 0.7 copy.33
  2.0 0.0 copy-start.3
  2.0 0.1 copy.26
  2.1 0.6 copy-done.9
  2.8 0.0 copy-start.2
  2.8 0.6 copy-done.11
  3.4 0.0 copy-start
  3.4 0.0 copy-start.1
  3.5 0.1 copy.25
  3.5 0.0 copy-done.10
  3.5 0.0 copy-start.4
  3.5 0.0 copy-start.5
  3.6 0.0 copy-start.7
  3.6 0.0 copy-start.8
  3.6 0.1 copy.27.rcell
  3.7 0.0 copy-done.6
  3.7 0.0 copy-done.3
  3.7 0.0 copy-done.2
  3.8 0.6 copy-done
  4.3 0.1 copy-done.1
  4.4 0.0 copy-done.4
  4.4 0.0 copy-done.7
  4.4 70.8 %shard_map.181 = (bf16[1,8,64,128]{3,2,1,0:T(8,128)(2,1)S(1)}, f32[8,2,128]{2,1,0:T(2,128)S(1)}, f32[16,128]{1,0:T(8,128)S(1)}) custom-call(bf16[1,8,64,128]{3,2,1,0:T(8,128)(2,1)S(1)} %copy-done, bf16[1,8,64,128]{3,2,1,0:T(8,128)(2,1)S(1)} %copy-done.1, bf16[1,8,64,128]{3,2,1,0:T(8,128)(2,1)S(1)} %copy-done.2, bf16[1,8,64,128]{3,2,1,0:T(8,128)(2,1)S(1)} %copy-done.3, ...), custom_call_target="tpu_custom_call" | custom-call | tf_op jit(solution)/shard_map/pallas_call | solution.py:478
  75.2 0.6 slice.40
  75.8 0.7 slice_reduce_fusion
  76.5 0.1 slice.39
  76.5 0.1 copy.30
  76.6 0.6 reshape.76
  77.3 0.1 copy.28
  77.4 0.6 copy.31
  78.0 0.7 copy.37
  78.6 0.6 copy.38
  (13 shorter events, 0.1 us)
Async XLA Ops:
  2.0 0.7 copy-start.9
  2.0 1.5 %copy-start.10 = (s32[1,256,2]{1,2,0:T(2,128)S(1)}, s32[1,256,2]{1,2,0:T(2,128)}, u32[]{:S(2)}) copy-start(s32[1,256,2]{1,2,0:T(2,128)} %param.24) | copy-start | bytes 6148
  2.0 1.7 %copy-start.6 = (f32[1,2,256]{2,1,0:T(2,128)S(1)}, f32[1,2,256]{2,1,0:T(2,128)}, u32[]{:S(2)}) copy-start(f32[1,2,256]{2,1,0:T(2,128)} %rtrace.1) | copy-start | bytes 6148
  2.0 1.7 %copy-start.3 = (bf16[1,8,64,128]{3,2,1,0:T(8,128)(2,1)S(1)}, bf16[1,8,64,128]{3,2,1,0:T(8,128)(2,1)}, u32[]{:S(2)}) copy-start(bf16[1,8,64,128]{3,2,1,0:T(8,128)(2,1)} %an.1) | copy-start | bytes 393220
  2.7 0.7 copy-start.11
  2.8 1.0 %copy-start.2 = (bf16[1,8,64,128]{3,2,1,0:T(8,128)(2,1)S(1)}, bf16[1,8,64,128]{3,2,1,0:T(8,128)(2,1)}, u32[]{:S(2)}) copy-start(bf16[1,8,64,128]{3,2,1,0:T(8,128)(2,1)} %ab.1) | copy-start | bytes 393220
  3.4 0.9 %copy-start = (bf16[1,8,64,128]{3,2,1,0:T(8,128)(2,1)S(1)}, bf16[1,8,64,128]{3,2,1,0:T(8,128)(2,1)}, u32[]{:S(2)}) copy-start(bf16[1,8,64,128]{3,2,1,0:T(8,128)(2,1)} %wb.1) | copy-start | bytes 393220
  3.4 1.0 %copy-start.1 = (bf16[1,8,64,128]{3,2,1,0:T(8,128)(2,1)S(1)}, bf16[1,8,64,128]{3,2,1,0:T(8,128)(2,1)}, u32[]{:S(2)}) copy-start(bf16[1,8,64,128]{3,2,1,0:T(8,128)(2,1)} %wn.1) | copy-start | bytes 393220
  3.5 0.9 %copy-start.4 = (f32[8,2,128]{2,1,0:T(2,128)S(1)}, f32[8,2,128]{2,1,0:T(2,128)}, u32[]{:S(2)}) copy-start(f32[8,2,128]{2,1,0:T(2,128)} %vel.1) | copy-start | bytes 24580
  3.5 0.9 %copy-start.5 = (f32[8,2,128]{2,1,0:T(2,128)S(1)}, f32[8,2,128]{2,1,0:T(2,128)}, u32[]{:S(2)}) copy-start(f32[8,2,128]{2,1,0:T(2,128)} %tgt.1) | copy-start | bytes 24580
  3.6 0.8 %copy-start.7 = (s32[1,3]{1,0:T(1,128)S(1)}, s32[1,3]{1,0:T(1,128)}, u32[]{:S(2)}) copy-start(s32[1,3]{1,0:T(1,128)} %scell.1) | copy-start | bytes 40
  3.6 0.8 %copy-start.8 = (f32[1,2]{1,0:T(1,128)S(1)}, f32[1,2]{1,0:T(1,128)}, u32[]{:S(2)}) copy-start(f32[1,2]{1,0:T(1,128)} %swave.1) | copy-start | bytes 28

commit v2 on v1

--- a/solution.py
+++ b/solution.py
@@ -55,11 +55,12 @@
 
 
 def kernel(
-    wb, wn, ab, an, vel, tgt, scell, swave, rcell, rtrace, wpack, b2,
+    wb_in, wn_in, ab_in, an_in, vel_in, tgt_in, scell_in, swave_in, rcell_in, rtrace_in, w1_in, b1_in, k2_in, b2_in,
     nw, nv, moves,
-    p0, q0, p1, q1, lap0, imgacc, vfull, vg, surf, imgt, ra, acca, rb, hb_img, hb_vel,
-    ext, gs, g2, rs, r2, fhi, flo, hid, smat, tt, mask, re,
-    s_hal, r_hal, s_v1, r_v1, s_v2, r_v2, s_hv, r_hv, s_a, r_a, s_b, r_b, s_c, r_c, s_e, r_e,
+    wb, wn, ab, an, vel, tgt, scell, swave, rcell, rtrace, w1_own, b1, k2_own, b2,
+    p0, q0, p1, q1, lap0, lapq, imgacc, vfull, vg, surf, imgt, ra, acca, rb, hb_img, hb_vel,
+    ext, gs, g2, rs, r2, fhi, flo, hid, smat, tt, mask, re, wt, kt,
+    s_in, s_hal, r_hal, s_v1, r_v1, s_v2, r_v2, s_hv, r_hv, s_a, r_a, s_b, r_b, s_c, r_c, s_e, r_e,
 ):
     shot = lax.axis_index("shot")
     sub = lax.axis_index("sub")
@@ -97,7 +98,23 @@
     for device in greeted:
         pl.semaphore_signal(barrier, inc=1, device_id=device, device_id_type=MESH)
 
+    loads = [
+        pltpu.make_async_copy(outer, inner, s_in.at[n])
+        for n, (outer, inner) in enumerate((
+            (wn_in, wn), (an_in, an), (vel_in, vel), (wb_in, wb), (ab_in, ab), (rcell_in, rcell),
+            (rtrace_in, rtrace), (scell_in, scell), (swave_in, swave), (tgt_in, tgt), (w1_in, w1_own),
+            (b1_in, b1), (k2_in, k2_own), (b2_in, b2),
+        ))
+    ]
+    for copy in loads:
+        copy.start()
+
     pending = []
+
+    def settle(keep=0):
+        for copy in pending[: len(pending) - keep]:
+            copy.wait_send()
+        del pending[: len(pending) - keep]
 
     def send(src, dst, ssem, rsem, device):
         copy = pltpu.make_async_remote_copy(
@@ -111,26 +128,31 @@
     for field in (p0, q0, p1, q1):
         field[:, 0:PAD, :] = zeros_pad
         field[:, PAD + COLS :, :] = zeros_pad
+    loads[0].wait()
     p0[4:12, PAD : PAD + COLS, :] = wn[0].astype(F32)
+    loads[1].wait()
     q0[4:12, PAD : PAD + COLS, :] = an[0].astype(F32)
+    loads[2].wait()
     for j in range(2):
         hb_vel[4, j * 8 : (j + 1) * 8, :] = vel[:, j, :]
     own = pl.ds(pl.multiple_of(xc * 16, 16), 16)
-    vg[zh, own, :] = hb_vel[4]
+    vg[0, own, :] = hb_vel[4]
 
     pl.semaphore_wait(barrier, len(greeted))
 
-    def halo(field, index):
-        inner = pl.ds(PAD, COLS)
-        a = send(
-            field.at[pl.ds(8, 4), inner, :], field.at[pl.ds(0, 4), inner, :],
-            s_hal.at[index], r_hal.at[index], (shot, up),
-        )
-        b = send(
-            field.at[pl.ds(4, 4), inner, :], field.at[pl.ds(12, 4), inner, :],
-            s_hal.at[index + 1], r_hal.at[index + 1], (shot, down),
-        )
-        return a, b
+    every = pl.ds(PAD, COLS)
+
+    def halo(field, index, columns=every):
+        return [
+            send(
+                field.at[pl.ds(8, 4), columns, :], field.at[pl.ds(0, 4), columns, :],
+                s_hal.at[index], r_hal.at[index], (shot, up),
+            ),
+            send(
+                field.at[pl.ds(4, 4), columns, :], field.at[pl.ds(12, 4), columns, :],
+                s_hal.at[index + 1], r_hal.at[index + 1], (shot, down),
+            ),
+        ]
 
     def halo_wait(field, copies):
         for copy in copies:
@@ -144,15 +166,10 @@
         def _():
             field[12:16, PAD : PAD + COLS, :] = jnp.zeros((4, COLS, DEPTH), F32)
 
+    behind = (0, 1, 3, 2)
     v1 = [
-        send(hb_vel.at[4], vg.at[zh, own, :], s_v1.at[k - 1], r_v1.at[k - 1], zh_peer(k)) for k in range(1, 4)
-    ]
-    halo_p0 = halo(p0, 0)
-    halo_q0 = halo(q0, 2)
-    for copy in v1:
-        copy.wait_recv()
-    v2 = [
-        send(vg.at[:, own, :], vg.at[:, own, :], s_v2.at[k - 1], r_v2.at[k - 1], xc_peer(k)) for k in range(1, 8)
+        send(hb_vel.at[4], vg.at[slot, own, :], s_v1.at[slot - 1], r_v1.at[slot - 1], zh_peer(behind[slot]))
+        for slot in (3, 1, 2)
     ]
 
     def around_sends(buffer, ssem, rsem):
@@ -163,25 +180,126 @@
             for n, (d, e) in enumerate(around)
         ]
 
-    hv = around_sends(hb_vel, s_hv, r_hv)
-
-    cells = rcell[0].astype(F32).astype(BF16)
-    pick = (
-        lax.broadcasted_iota(jnp.int32, (8, 2), 0) == lax.broadcasted_iota(jnp.int32, (8, 2), 1)
-    ).astype(F32).astype(BF16)
-    cells_t = dot_t(pick, cells)
-    rec_x = cells_t[0:1, :]
-    rec_y = cells_t[1:2, :]
+    for copy in loads[3:9]:
+        copy.wait()
+    cells = rcell[0].astype(F32)
     hit_y = (
-        lax.broadcasted_iota(jnp.int32, (COLS, 256), 0).astype(F32) == jnp.broadcast_to(rec_y, (COLS, 256))
+        lax.broadcasted_iota(jnp.int32, (COLS, 256), 0).astype(F32) == jnp.broadcast_to(cells[1:2], (COLS, 256))
     ).astype(F32).astype(BF16)
     rows_here = (lax.broadcasted_iota(jnp.int32, (8, 256), 0) + x0).astype(F32)
-    hit_x = (rows_here == jnp.broadcast_to(rec_x, (8, 256))).astype(F32)
+    hit_x = (rows_here == jnp.broadcast_to(cells[0:1], (8, 256))).astype(F32)
     trace = jnp.concatenate([hit_x * rtrace[0, 0:1, :], hit_x * rtrace[0, 1:2, :]], axis=0)
     t_hi, t_rest = trace.astype(BF16), trace - trace.astype(BF16).astype(F32)
     t_mid, t_lo = halves(t_rest)
     surf[:, 0:16] = dot_t(hit_y, t_hi) + dot_t(hit_y, t_mid) + dot_t(hit_y, t_lo)
 
+    z_row = lax.broadcasted_iota(jnp.int32, (COLS, DEPTH), 1)
+    y_row = lax.broadcasted_iota(jnp.int32, (COLS, DEPTH), 0)
+    source_cell = [jnp.broadcast_to(scell[0:1, n : n + 1], (COLS, DEPTH)) for n in range(3)]
+    source_yz = (y_row == source_cell[1]) & (z_row == source_cell[2])
+    source_amount = [
+        jnp.where(source_yz, jnp.broadcast_to(swave[0:1, n : n + 1], (COLS, DEPTH)), 0.0) for n in range(2)
+    ]
+    rec_mark = z_row == ZREC
+    back_w = [None] + [jnp.where(z_row[0:8] >= k, COEFFS[k], 0.0) for k in range(1, 5)]
+    fore_w = [None] + [jnp.where(z_row[0:8] < DEPTH - k, COEFFS[k], 0.0) for k in range(1, 5)]
+
+    def tall(w):
+        return jnp.broadcast_to(w[0:1], (COLS, DEPTH))
+
+    def lap_row(field, i):
+        center = field[i + 4, every, :]
+        out = (3.0 * COEFFS[0]) * center
+        for k in range(1, 5):
+            out = out + COEFFS[k] * (
+                (field[i + 4 + k, every, :] + field[i + 4 - k, every, :])
+                + (field[i + 4, pl.ds(PAD + k, COLS), :] + field[i + 4, pl.ds(PAD - k, COLS), :])
+            )
+            out = out + pltpu.roll(center, k, 1) * tall(back_w[k])
+            out = out + pltpu.roll(center, DEPTH - k, 1) * tall(fore_w[k])
+        return center, out
+
+    def source(i, step):
+        return jnp.where(source_cell[0] == x0 + i, source_amount[step], 0.0)
+
+    def receivers(i, step):
+        column = pltpu.roll(surf[...], (DEPTH + ZREC - step * 8 - i) % DEPTH, 1)
+        return jnp.where(rec_mark, column, 0.0)
+
+    for copy in v1:
+        copy.wait_recv()
+    v2 = [
+        send(vg.at[:, own, :], vg.at[:, own, :], s_v2.at[k - 1], r_v2.at[k - 1], xc_peer(k)) for k in range(1, 8)
+    ]
+
+    halo_p0 = halo(p0, 0)
+    halo_q0 = halo(q0, 2)
+    halo_wait(p0, halo_p0)
+
+    def forward_0(i, carry):
+        center, lap = lap_row(p0, i)
+        lap0[i] = lap
+        p1[i + 4, every, :] = 2.0 * center - wb[0, i].astype(F32) + source(i, 0)
+        return carry
+
+    lax.fori_loop(0, ROWS, forward_0, 0)
+
+    def adjoint_0(i, carry):
+        center, lap = lap_row(q0, i)
+        lapq[i] = lap
+        q1[i + 4, every, :] = 2.0 * center - ab[0, i].astype(F32) + receivers(i, 0)
+        return carry
+
+    halo_wait(q0, halo_q0)
+    lax.fori_loop(0, ROWS, adjoint_0, 0)
+
+    for copy in v2:
+        copy.wait_recv()
+    for slot in range(4):
+        columns = pl.ds(pl.multiple_of(((zh + 4 - behind[slot]) % 4) * 16, 16), 16)
+        for i in range(ROWS):
+            vfull[i, columns, :] = vg.at[slot][pl.ds(i, 16, stride=8), :]
+    p1[4:12, every, :] = p1[4:12, every, :] + vfull[...] * lap0[...]
+    halo_p1 = halo(p1, 4)
+    q1[4:12, every, :] = q1[4:12, every, :] + vfull[...] * lapq[...]
+    halo_q1 = halo(q1, 6)
+    hv = around_sends(hb_vel, s_hv, r_hv)
+
+    halo_wait(p1, halo_p1)
+
+    def forward_1(i, carry):
+        center, lap = lap_row(p1, i)
+        fresh = 2.0 * center - p0[i + 4, every, :] + vfull[i] * lap + source(i, 1)
+        nw[0, i] = fresh.astype(BF16)
+        imgacc[i] = lap * q1[i + 4, every, :]
+        return carry
+
+    lax.fori_loop(0, ROWS, forward_1, 0)
+
+    halo_wait(q1, halo_q1)
+
+    def adjoint_1(i, carry):
+        center, lap = lap_row(q1, i)
+        fresh = 2.0 * center - q0[i + 4, every, :] + vfull[i] * lap + receivers(i, 1)
+        imgacc[i] = imgacc[i] + lap0[i] * fresh
+        return carry
+
+    lax.fori_loop(0, ROWS, adjoint_1, 0)
+    for z in range(4):
+        for i in range(ROWS):
+            imgt.at[z][pl.ds(i, 16, stride=8), :] = imgacc[i, z * 16 : (z + 1) * 16, :]
+
+    sends_a = [
+        send(
+            imgt.at[:, pl.ds(pl.multiple_of(((xc + k) % 8) * 16, 16), 16), :], ra.at[k - 1],
+            s_a.at[k - 1], r_a.at[k - 1], xc_peer(k),
+        )
+        for k in range(1, 8)
+    ]
+    settle(7)
+
+    for copy in loads[9:]:
+        copy.wait()
     lane = lax.broadcasted_iota(jnp.int32, (16, HID), 1)
     tile = lane >> 7
     hid_y = (tile >= 12).astype(jnp.int32) + (tile >= 24).astype(jnp.int32) + (tile >= 36).astype(jnp.int32)
@@ -193,68 +311,6 @@
     ).astype(F32)
     gs[...] = jnp.where(lax.broadcasted_iota(jnp.int32, (TILES * 8, DEPTH), 0) % 8 == 6, 1.0, 0.0)
     rs[...] = jnp.zeros((TILES * 8, DEPTH), F32)
-
-    z_row = lax.broadcasted_iota(jnp.int32, (COLS, DEPTH), 1)
-    y_row = lax.broadcasted_iota(jnp.int32, (COLS, DEPTH), 0)
-    source_yz = jnp.where((y_row == scell[0, 1]) & (z_row == scell[0, 2]), 1.0, 0.0)
-    rec_mark = z_row == ZREC
-    back_w = [None] + [jnp.where(z_row[0:8] >= k, COEFFS[k], 0.0) for k in range(1, 5)]
-    fore_w = [None] + [jnp.where(z_row[0:8] < DEPTH - k, COEFFS[k], 0.0) for k in range(1, 5)]
-
-    def tall(w):
-        return jnp.broadcast_to(w[0:1], (COLS, DEPTH))
-
-    def lap_row(field, i):
-        inner = pl.ds(PAD, COLS)
-        center = field[i + 4, inner, :]
-        out = (3.0 * COEFFS[0]) * center
-        for k in range(1, 5):
-            out = out + COEFFS[k] * (
-                (field[i + 4 + k, inner, :] + field[i + 4 - k, inner, :])
-                + (field[i + 4, pl.ds(PAD + k, COLS), :] + field[i + 4, pl.ds(PAD - k, COLS), :])
-            )
-            out = out + pltpu.roll(center, k, 1) * tall(back_w[k])
-            out = out + pltpu.roll(center, DEPTH - k, 1) * tall(fore_w[k])
-        return center, out
-
-    def source(i, step):
-        amount = jnp.where(scell[0, 0] == x0 + i, swave[0, step], 0.0)
-        return amount * source_yz
-
-    def receivers(i, step):
-        column = pltpu.roll(surf[...], (DEPTH + ZREC - step * 8 - i) % DEPTH, 1)
-        return jnp.where(rec_mark, column, 0.0)
-
-    for copy in v2:
-        copy.wait_recv()
-    for z in range(4):
-        for i in range(ROWS):
-            vfull[i, z * 16 : (z + 1) * 16, :] = vg.at[z][pl.ds(i, 16, stride=8), :]
-    halo_wait(p0, halo_p0)
-
-    def forward_0(i, carry):
-        center, lap = lap_row(p0, i)
-        lap0[i] = lap
-        p1[i + 4, pl.ds(PAD, COLS), :] = (
-            2.0 * center - wb[0, i].astype(F32) + vfull[i] * lap + source(i, 0)
-        )
-        return carry
-
-    lax.fori_loop(0, ROWS, forward_0, 0)
-    halo_p1 = halo(p1, 4)
-
-    halo_wait(q0, halo_q0)
-
-    def adjoint_0(i, carry):
-        center, lap = lap_row(q0, i)
-        q1[i + 4, pl.ds(PAD, COLS), :] = (
-            2.0 * center - ab[0, i].astype(F32) + vfull[i] * lap + receivers(i, 0)
-        )
-        return carry
-
-    lax.fori_loop(0, ROWS, adjoint_0, 0)
-    halo_q1 = halo(q1, 6)
-
     ok_shot = {-1: shot > 0, 0: None, 1: shot < N_SHOT - 1}
     ok_sub = {-1: sub > 0, 0: None, 1: sub < N_SUB - 1}
 
@@ -283,37 +339,26 @@
         copy.wait_recv()
     channel(hb_vel, 1, True)
 
-    halo_wait(p1, halo_p1)
-
-    def forward_1(i, carry):
-        center, lap = lap_row(p1, i)
-        fresh = 2.0 * center - p0[i + 4, pl.ds(PAD, COLS), :] + vfull[i] * lap + source(i, 1)
-        nw[0, i] = fresh.astype(BF16)
-        imgacc[i] = lap * q1[i + 4, pl.ds(PAD, COLS), :]
-        return carry
-
-    lax.fori_loop(0, ROWS, forward_1, 0)
-
-    halo_wait(q1, halo_q1)
-
-    def adjoint_1(i, carry):
-        center, lap = lap_row(q1, i)
-        fresh = 2.0 * center - q0[i + 4, pl.ds(PAD, COLS), :] + vfull[i] * lap + receivers(i, 1)
-        imgacc[i] = imgacc[i] + lap0[i] * fresh
-        return carry
-
-    lax.fori_loop(0, ROWS, adjoint_1, 0)
-    for z in range(4):
-        for i in range(ROWS):
-            imgt.at[z][pl.ds(i, 16, stride=8), :] = imgacc[i, z * 16 : (z + 1) * 16, :]
-
-    sends_a = [
-        send(
-            imgt.at[:, pl.ds(pl.multiple_of(((xc + k) % 8) * 16, 16), 16), :], ra.at[k - 1],
-            s_a.at[k - 1], r_a.at[k - 1], xc_peer(k),
-        )
-        for k in range(1, 8)
-    ]
+    wt[...] = jnp.zeros((80, DEPTH), F32)
+    kt[...] = jnp.zeros((80, DEPTH), F32)
+    for n in range(9):
+        for i in range(2):
+            wt[n * 8 + i * 3 : n * 8 + i * 3 + 3, 0:16] = w1_own[n // 3, n % 3, :, i, :]
+        kt[n * 8 : n * 8 + 3, 0:16] = k2_own[n // 3, n % 3, :, 0, :]
+    wt[38:39, 0:16] = b1[...]
+    w1_hi, w1_lo = halves(wt[:, 0:16])
+    k2_hi, k2_lo = halves(kt[:, 0:16])
+    unit = (
+        lax.broadcasted_iota(jnp.int32, (16, 16), 0) == lax.broadcasted_iota(jnp.int32, (16, 16), 1)
+    ).astype(F32).astype(BF16)
+
+    def turn(x):
+        return dot_t(unit, x).astype(BF16)
+
+    w1_cat = jnp.concatenate([turn(w1_hi), turn(w1_hi), turn(w1_lo)], axis=1)
+    k2_cat = jnp.concatenate([turn(k2_hi), turn(k2_hi), turn(k2_lo)], axis=1)
+    k2t_cat = jnp.concatenate([k2_hi, k2_hi, k2_lo], axis=1)
+
     total = imgt[:, own, :]
     for k in range(1, 8):
         sends_a[k - 1].wait_recv()
@@ -322,6 +367,7 @@
     sends_b = [
         send(acca.at[(zh + k) % 4], rb.at[k - 1], s_b.at[k - 1], r_b.at[k - 1], zh_peer(k)) for k in range(1, 4)
     ]
+    settle(3)
     total = acca[zh]
     for k in range(1, 4):
         sends_b[k - 1].wait_recv()
@@ -329,18 +375,7 @@
     hb_img[4] = total * (1.0 / N_SHOT)
     sends_c = around_sends(hb_img, s_c, r_c)
 
-    w1, k2 = wpack[:, 0:80], wpack[:, 128:208]
-    w1_hi, w1_lo = halves(w1)
-    k2_hi, k2_lo = halves(k2)
-    w1_cat = jnp.concatenate([w1_hi, w1_hi, w1_lo], axis=1)
-    k2_cat = jnp.concatenate([k2_hi, k2_hi, k2_lo], axis=1)
-    unit = (
-        lax.broadcasted_iota(jnp.int32, (80, 80), 0) == lax.broadcasted_iota(jnp.int32, (80, 80), 1)
-    ).astype(F32).astype(BF16)
-    k2t_hi = dot_t(unit, k2_hi).astype(BF16)
-    k2t_lo = dot_t(unit, k2_lo).astype(BF16)
-    k2t_cat = jnp.concatenate([k2t_hi, k2t_hi, k2t_lo], axis=1)
-
+    settle(8)
     for copy in sends_c:
         copy.wait_recv()
     channel(hb_img, 0, False)
@@ -421,6 +456,7 @@
             )
             for k in range(1, 8)
         ]
+        settle(7)
         for copy in copies:
             copy.wait_recv()
         pack = re[level, 0]
@@ -431,27 +467,49 @@
     factor = 1.0 / jnp.sqrt(squares * (1.0 / ENTRIES) + 1e-06)
     moves[...] = pack * factor
 
-    for copy in pending:
-        copy.wait_send()
+    settle()
+
+
+def writer(nw, nv, moves, nw_out, nv_out, w1_out, b1_out, k2_out, b2_out, nw_own, nv_own, pack, w1_own, k2_own, sem):
+    def copy(source, target, n):
+        move = pltpu.make_async_copy(source, target, sem.at[n])
+        move.start()
+        return move
+
+    loads = [copy(moves, pack, 0), copy(nw, nw_own, 1), copy(nv, nv_own, 2)]
+    loads[0].wait()
+    turned = jnp.transpose(pack[...])
+    for n in range(9):
+        for i in range(2):
+            w1_own[n // 3, n % 3, :, i, :] = turned[n * 8 + i * 3 : n * 8 + i * 3 + 3]
+        k2_own[n // 3, n % 3, :, 0, :] = turned[72 + 3 * n : 75 + 3 * n]
+    b1_out[...] = turned[38:39]
+    b2_out[...] = pack[0:1, 99:100]
+    stores = [copy(w1_own, w1_out, 3), copy(k2_own, k2_out, 4)]
+    loads[1].wait()
+    stores.append(copy(nw_own, nw_out, 5))
+    loads[2].wait()
+    stores.append(copy(nv_own, nv_out, 6))
+    for move in stores:
+        move.wait()
 
 
 def shards(
     wave_before, wave_now, adjoint_before, adjoint_now, velocity, target_model, source_cell, source_wave,
     receiver_cell, receiver_trace, first_kernel, first_bias, second_kernel, second_bias,
 ):
-    w1 = first_kernel.transpose(0, 2, 3, 1, 4).reshape(16, 9, 6)
-    bias = jnp.zeros((16, 9, 1), F32).at[:, 4, 0].set(first_bias)
-    w1 = jnp.pad(jnp.concatenate([w1, bias], axis=2), ((0, 0), (0, 0), (0, 1))).reshape(16, 72)
-    k2 = jnp.pad(second_kernel.reshape(16, 9, 3), ((0, 0), (0, 0), (0, 5))).reshape(16, 72)
-    wpack = jnp.concatenate([jnp.pad(w1, ((0, 0), (0, 56))), jnp.pad(k2, ((0, 0), (0, 56)))], axis=1)
-
+    operands = (
+        wave_before, wave_now, adjoint_before, adjoint_now, velocity, target_model, source_cell, source_wave,
+        receiver_cell.transpose(0, 2, 1), receiver_trace, first_kernel.transpose(2, 3, 4, 1, 0),
+        first_bias.reshape(1, 16), second_kernel.transpose(2, 3, 4, 0, 1), second_bias,
+    )
     vmem = pl.BlockSpec(memory_space=pltpu.VMEM)
-    smem = pl.BlockSpec(memory_space=pltpu.SMEM)
+    hbm = pl.BlockSpec(memory_space=pltpu.HBM)
     dma = pltpu.SemaphoreType.DMA
     field = pltpu.VMEM((16, COLS + 2 * PAD, DEPTH), F32)
     block = pltpu.VMEM((ROWS, COLS, DEPTH), F32)
-    scratch = [
-        field, field, field, field, block, block, block,
+    scratch = [pltpu.VMEM(x.shape, x.dtype) for x in operands[:-1]] + [pltpu.SMEM((1,), F32)] + [
+        field, field, field, field, block, block, block, block,
         pltpu.VMEM((4, DEPTH, DEPTH), F32),
         pltpu.VMEM((COLS, DEPTH), F32),
         pltpu.VMEM((4, DEPTH, DEPTH), F32),
@@ -472,6 +530,9 @@
         pltpu.VMEM((160, DEPTH), F32),
         pltpu.VMEM((16, HID), F32),
         pltpu.VMEM((3, 8, 16, DEPTH), F32),
+        pltpu.VMEM((80, DEPTH), F32),
+        pltpu.VMEM((80, DEPTH), F32),
+        dma((len(operands),)),
     ]
     for count in (8, 3, 7, 8, 7, 3, 8, 21):
         scratch += [dma((count,)), dma((count,))]
@@ -482,25 +543,38 @@
             jax.ShapeDtypeStruct(velocity.shape, F32),
             jax.ShapeDtypeStruct((16, DEPTH), F32),
         ),
-        in_specs=[vmem, vmem, vmem, vmem, vmem, vmem, smem, smem, vmem, vmem, vmem, smem],
+        in_specs=[hbm] * len(operands),
         out_specs=(vmem, vmem, vmem),
         scratch_shapes=scratch,
         compiler_params=pltpu.CompilerParams(
-            collective_id=0, has_side_effects=True, vmem_limit_bytes=40 * 1024 * 1024
+            collective_id=0, has_side_effects=True, vmem_limit_bytes=60 * 1024 * 1024
         ),
-    )(
-        wave_before, wave_now, adjoint_before, adjoint_now, velocity, target_model, source_cell, source_wave,
-        receiver_cell, receiver_trace, wpack, second_bias,
+    )(*operands)
+    outs = (
+        jax.ShapeDtypeStruct(wave_now.shape, BF16),
+        jax.ShapeDtypeStruct(velocity.shape, F32),
+        jax.ShapeDtypeStruct((3, 3, 3, 2, 16), F32),
+        jax.ShapeDtypeStruct((1, 16), F32),
+        jax.ShapeDtypeStruct((3, 3, 3, 1, 16), F32),
+        jax.ShapeDtypeStruct((1, 1), F32),
     )
-    taps = moves[:, 0:72].reshape(16, 3, 3, 8)
-    first_move = taps[..., 0:6].reshape(16, 3, 3, 2, 3).transpose(0, 3, 1, 2, 4)
+    next_wave, new_velocity, w1, b1, k2, b2 = pl.pallas_call(
+        writer,
+        out_shape=outs,
+        in_specs=[hbm, hbm, hbm],
+        out_specs=(hbm, hbm, hbm, vmem, hbm, vmem),
+        scratch_shapes=[
+            pltpu.VMEM(outs[0].shape, BF16), pltpu.VMEM(outs[1].shape, F32), pltpu.VMEM((16, DEPTH), F32),
+            pltpu.VMEM(outs[2].shape, F32), pltpu.VMEM(outs[4].shape, F32), dma((7,)),
+        ],
+    )(next_wave, new_velocity, moves)
     return (
         next_wave,
         new_velocity,
-        first_move,
-        moves[:, 38],
-        moves[:, 72:99].reshape(1, 16, 3, 3, 3),
-        moves[0, 99:100],
+        w1.transpose(4, 3, 0, 1, 2),
+        b1.reshape(16),
+        k2.transpose(3, 4, 0, 1, 2),
+        b2.reshape(1),
     )
 
 

time: 79.8 us -> 71.3 us (0.89)
  local copies, waits for them, and re-layouts: 7 us -> 0 us
  Pallas kernels: 70.8 us -> 69.7 us
    unnamed x29 -> x0, local copies, waits for them, and re-layouts: 4.68 us -> none
    pallas_call x1, Pallas kernels: 70.8 us -> 67.5 us  [shards(): pl.pallas_call(kernel, out_shape=(jax.ShapeDtypeStruct(wave_now.shape, BF...]
    pallas_call x0 -> x1, Pallas kernels: none -> 2.15 us  [shards(): pl.pallas_call(writer, out_shape=outs, in_specs=[hbm, hbm, hbm], out_spec...]
    slice x6 -> x0, local copies, waits for them, and re-layouts: 1.53 us -> none  [the longest x1 0.69 us: shards(): moves[:, 38]]
where the time goes in v2:
time: 71.3 us; the launch traced here: 71 us
  Pallas kernels  69.7 us (98%)
  between operations  1.29 us (2%)
    pallas_call x1, Pallas kernels, shards(): pl.pallas_call(kernel, out_shape=(jax.ShapeDtypeStruct(wave_now.shape, BF...  67.5 us
    pallas_call x1, Pallas kernels, shards(): pl.pallas_call(writer, out_shape=outs, in_specs=[hbm, hbm, hbm], out_spec...  2.15 us

profile of v2, /device:TPU:1, one launch (start us, length us, event | category | flops | bytes accessed | tf_op | source)
XLA Modules:
  0.0 71.0 jit_solution(825246544788231852)
XLA Ops:
  1.3 67.5 %shard_map.181 = (bf16[1,8,64,128]{3,2,1,0:T(8,128)(2,1)}, f32[8,2,128]{2,1,0:T(2,128)}, f32[16,128]{1,0:T(8,128)}) custom-call(bf16[1,8,64,128]{3,2,1,0:T(8,128)(2,1)} %wb_in.1, bf16[1,8,64,128]{3,2,1,0:T(8,128)(2,1)} %wn_in.1, bf16[1,8,64,128]{3,2,1,0:T(8,128)(2,1)} %ab_in.1, bf16[1,8,64,128]{3,2,1,0:T(8,128)(2,1)} %an_in.1, f32[8,2,128]{2,1,0:T(2,128)} %vel_in.1, ...), custom_call_target="tpu_custom_call" | custom-call | tf_op jit(solution)/shard_map/pallas_call | solution.py:539
  68.8 2.2 %shard_map.182 = (bf16[1,8,64,128]{3,2,1,0:T(8,128)(2,1)}, f32[8,2,128]{2,1,0:T(2,128)}, f32[3,3,3,2,16]{4,3,2,1,0:T(2,128)}, f32[1,16]{1,0:T(1,128)}, f32[3,3,3,1,16]{4,3,2,1,0:T(1,128)}, /*index=5*/f32[1,1]{1,0:T(1,128)}) custom-call(bf16[1,8,64,128]{3,2,1,0:T(8,128)(2,1)} %get-tuple-element.15.nw, f32[8,2,128]{2,1,0:T(2,128)} %get-tuple-element.16.nv, ...), custom_call_target="tpu_custom_call" | custom-call | tf_op jit(solution)/shard_map/pallas_call | solution.py:561

commit v3 on v2

--- a/solution.py
+++ b/solution.py
@@ -58,42 +58,43 @@
     wb_in, wn_in, ab_in, an_in, vel_in, tgt_in, scell_in, swave_in, rcell_in, rtrace_in, w1_in, b1_in, k2_in, b2_in,
     nw, nv, moves,
     wb, wn, ab, an, vel, tgt, scell, swave, rcell, rtrace, w1_own, b1, k2_own, b2,
-    p0, q0, p1, q1, lap0, lapq, imgacc, vfull, vg, surf, imgt, ra, acca, rb, hb_img, hb_vel,
+    p0, q0, p1, q1, lap0, lapq, imgacc, vfull, vg, surf, imgt, ra, acca, edge, whole, sides, hb_vel,
     ext, gs, g2, rs, r2, fhi, flo, hid, smat, tt, mask, re, wt, kt,
-    s_in, s_hal, r_hal, s_v1, r_v1, s_v2, r_v2, s_hv, r_hv, s_a, r_a, s_b, r_b, s_c, r_c, s_e, r_e,
+    s_in, s_hal, r_hal, s_v1, r_v1, s_v2, r_v2, s_hv, r_hv, s_a, r_a, s_b, r_b, s_e, r_e,
 ):
     shot = lax.axis_index("shot")
     sub = lax.axis_index("sub")
-    zh, xc = shot // 8, shot % 8
-    zlo, yy = sub // 8, sub % 8
+    zh, xc = lax.div(shot, 8), lax.rem(shot, 8)
+    zlo, yy = lax.div(sub, 8), lax.rem(sub, 8)
     zz = zh * 2 + zlo
     x0 = sub * ROWS
-    up, down = (sub + 1) % N_SUB, (sub + N_SUB - 1) % N_SUB
+    up, down = lax.rem(sub + 1, N_SUB), lax.rem(sub + (N_SUB - 1), N_SUB)
 
     def xc_peer(k):
-        return (zh * 8 + (xc + k) % 8, sub)
+        return (zh * 8 + lax.rem(xc + k, 8), sub)
 
     def zh_peer(k):
-        return (((zh + k) % 4) * 8 + xc, sub)
+        return (lax.rem(zh + k, 4) * 8 + xc, sub)
 
     def z_peer(k):
-        z = (zz + k) % 8
-        return ((z // 2) * 8 + xc, (z % 2) * 8 + yy)
+        z = lax.rem(zz + k, 8)
+        return (lax.div(z, 2) * 8 + xc, lax.rem(z, 2) * 8 + yy)
 
     def y_peer(k):
-        return (shot, zlo * 8 + (yy + k) % 8)
+        return (shot, zlo * 8 + lax.rem(yy + k, 8))
 
     def near(d, e):
-        return ((shot + d + N_SHOT) % N_SHOT, (sub + e + N_SUB) % N_SUB)
+        return (lax.rem(shot + (d + N_SHOT), N_SHOT), lax.rem(sub + (e + N_SUB), N_SUB))
 
     around = [(d, e) for d in (-1, 0, 1) for e in (-1, 0, 1) if (d, e) != (0, 0)]
-    greeted = (
-        [near(d, e) for d, e in around]
-        + [xc_peer(k) for k in range(1, 8)]
-        + [zh_peer(k) for k in range(1, 4)]
-        + [z_peer(k) for k in range(1, 8)]
-        + [y_peer(k) for k in range(1, 8)]
-    )
+    def user(k, d, e):
+        owner = lax.rem(zh + k, 4) * 8 + xc
+        return (lax.rem(owner + (d + N_SHOT), N_SHOT), lax.rem(sub + (e + N_SUB), N_SUB))
+
+    users = [(k, d, e) for k in (2, 1, 3, 0) for d in (1, -1, 0) for e in (1, -1, 0) if (k, d, e) != (0, 0, 0)]
+    twin = (shot, lax.rem(sub + 8, N_SUB))
+    greeted = [xc_peer(k) for k in range(1, 8)] + [zh_peer(k) for k in range(1, 4)] + [twin]
+    greeted += [near(d, e) for d, e in around]
     barrier = pltpu.get_barrier_semaphore()
     for device in greeted:
         pl.semaphore_signal(barrier, inc=1, device_id=device, device_id_type=MESH)
@@ -101,7 +102,7 @@
     loads = [
         pltpu.make_async_copy(outer, inner, s_in.at[n])
         for n, (outer, inner) in enumerate((
-            (wn_in, wn), (an_in, an), (vel_in, vel), (wb_in, wb), (ab_in, ab), (rcell_in, rcell),
+            (vel_in, vel), (wn_in, wn), (an_in, an), (wb_in, wb), (ab_in, ab), (rcell_in, rcell),
             (rtrace_in, rtrace), (scell_in, scell), (swave_in, swave), (tgt_in, tgt), (w1_in, w1_own),
             (b1_in, b1), (k2_in, k2_own), (b2_in, b2),
         ))
@@ -124,19 +125,10 @@
         pending.append(copy)
         return copy
 
-    zeros_pad = jnp.zeros((16, PAD, DEPTH), F32)
-    for field in (p0, q0, p1, q1):
-        field[:, 0:PAD, :] = zeros_pad
-        field[:, PAD + COLS :, :] = zeros_pad
     loads[0].wait()
-    p0[4:12, PAD : PAD + COLS, :] = wn[0].astype(F32)
-    loads[1].wait()
-    q0[4:12, PAD : PAD + COLS, :] = an[0].astype(F32)
-    loads[2].wait()
     for j in range(2):
         hb_vel[4, j * 8 : (j + 1) * 8, :] = vel[:, j, :]
     own = pl.ds(pl.multiple_of(xc * 16, 16), 16)
-    vg[0, own, :] = hb_vel[4]
 
     pl.semaphore_wait(barrier, len(greeted))
 
@@ -171,6 +163,18 @@
         send(hb_vel.at[4], vg.at[slot, own, :], s_v1.at[slot - 1], r_v1.at[slot - 1], zh_peer(behind[slot]))
         for slot in (3, 1, 2)
     ]
+
+    vg[0, own, :] = hb_vel[4]
+
+    loads[1].wait()
+    p0[4:12, every, :] = wn[0].astype(F32)
+    halo_p0 = halo(p0, 0)
+    loads[2].wait()
+    q0[4:12, every, :] = an[0].astype(F32)
+    zeros_pad = jnp.zeros((16, PAD, DEPTH), F32)
+    for field in (p0, q0, p1, q1):
+        field[:, 0:PAD, :] = zeros_pad
+        field[:, PAD + COLS :, :] = zeros_pad
 
     def around_sends(buffer, ssem, rsem):
         return [
@@ -232,7 +236,6 @@
         send(vg.at[:, own, :], vg.at[:, own, :], s_v2.at[k - 1], r_v2.at[k - 1], xc_peer(k)) for k in range(1, 8)
     ]
 
-    halo_p0 = halo(p0, 0)
     halo_q0 = halo(q0, 2)
     halo_wait(p0, halo_p0)
 
@@ -256,7 +259,7 @@
     for copy in v2:
         copy.wait_recv()
     for slot in range(4):
-        columns = pl.ds(pl.multiple_of(((zh + 4 - behind[slot]) % 4) * 16, 16), 16)
+        columns = pl.ds(pl.multiple_of(lax.rem(zh + (4 - behind[slot]), 4) * 16, 16), 16)
         for i in range(ROWS):
             vfull[i, columns, :] = vg.at[slot][pl.ds(i, 16, stride=8), :]
     p1[4:12, every, :] = p1[4:12, every, :] + vfull[...] * lap0[...]
@@ -291,7 +294,7 @@
 
     sends_a = [
         send(
-            imgt.at[:, pl.ds(pl.multiple_of(((xc + k) % 8) * 16, 16), 16), :], ra.at[k - 1],
+            imgt.at[:, pl.ds(pl.multiple_of(lax.rem(xc + k, 8) * 16, 16), 16), :], ra.at[k - 1],
             s_a.at[k - 1], r_a.at[k - 1], xc_peer(k),
         )
         for k in range(1, 8)
@@ -314,30 +317,28 @@
     ok_shot = {-1: shot > 0, 0: None, 1: shot < N_SHOT - 1}
     ok_sub = {-1: sub > 0, 0: None, 1: sub < N_SUB - 1}
 
-    def channel(buffer, which, centered):
+    def channel(which, piece):
         for d in (-1, 0, 1):
             for e in (-1, 0, 1):
                 for j in range(2):
-                    block = buffer[(d + 1) * 3 + (e + 1), j * 8 : (j + 1) * 8, :]
-                    if centered:
-                        block = (block - CENTER_SHIFT) * CENTER_GAIN
+                    block = piece(d, e, j)
                     for ok in (ok_shot[d], ok_sub[e]):
                         if ok is not None:
                             block = block * jnp.where(ok, 1.0, 0.0)
-                    row = (2 + 2 * d + j) * WIDE
-                    if e == -1:
-                        ext[row : row + 2, :] = block[6:8]
-                    elif e == 0:
-                        ext[row + 2 : row + 10, :] = block
-                    else:
-                        ext[row + 10 : row + 12, :] = block[0:2]
+                    row = (2 + 2 * d + j) * WIDE + (0, 2, 10)[e + 1]
+                    ext[row : row + block.shape[0], :] = block
         value = ext[...]
         for dz in range(3):
             gs[pl.ds(which * 3 + dz, 72, stride=8), :] = shifted(value, dz - 1)
 
+    def velocity_piece(d, e, j):
+        first = j * 8 + (6 if e == -1 else 0)
+        block = hb_vel[(d + 1) * 3 + (e + 1), first : first + (8 if e == 0 else 2), :]
+        return (block - CENTER_SHIFT) * CENTER_GAIN
+
     for copy in hv:
         copy.wait_recv()
-    channel(hb_vel, 1, True)
+    channel(1, velocity_piece)
 
     wt[...] = jnp.zeros((80, DEPTH), F32)
     kt[...] = jnp.zeros((80, DEPTH), F32)
@@ -364,21 +365,33 @@
         sends_a[k - 1].wait_recv()
         total = total + ra[k - 1]
     acca[...] = total
-    sends_b = [
-        send(acca.at[(zh + k) % 4], rb.at[k - 1], s_b.at[k - 1], r_b.at[k - 1], zh_peer(k)) for k in range(1, 4)
-    ]
-    settle(3)
-    total = acca[zh]
-    for k in range(1, 4):
-        sends_b[k - 1].wait_recv()
-        total = total + rb[k - 1]
-    hb_img[4] = total * (1.0 / N_SHOT)
-    sends_c = around_sends(hb_img, s_c, r_c)
-
-    settle(8)
-    for copy in sends_c:
+    for side, first in enumerate((0, 6)):
+        for j in range(2):
+            edge[side, :, 2 * j : 2 * j + 2, :] = total[:, 8 * j + first : 8 * j + first + 2, :]
+    sends_b = []
+    for n, (k, d, e) in enumerate(users):
+        z = lax.rem(zh + k, 4)
+        source_ref = acca.at[z] if e == 0 else edge.at[(e + 1) // 2, z]
+        target_ref = whole.at[1 - d, k] if e == 0 else sides.at[(1 - e) // 2, 1 - d, k]
+        sends_b.append(send(source_ref, target_ref, s_b.at[n], r_b.at[n], user(k, d, e)))
+    whole[1, 0] = acca[zh]
+    settle(len(users))
+    for copy in sends_b:
         copy.wait_recv()
-    channel(hb_img, 0, False)
+    image, image_edge = {}, {}
+    for d in (-1, 0, 1):
+        parts = [whole[d + 1, k] for k in range(4)]
+        image[d] = ((parts[0] + parts[1]) + (parts[2] + parts[3])) * (1.0 / N_SHOT)
+        for e in (-1, 1):
+            parts = [sides[(e + 1) // 2, d + 1, k] for k in range(4)]
+            image_edge[d, e] = ((parts[0] + parts[1]) + (parts[2] + parts[3])) * (1.0 / N_SHOT)
+
+    def image_piece(d, e, j):
+        if e == 0:
+            return image[d][j * 8 : (j + 1) * 8]
+        return image_edge[d, e][j * 2 : (j + 1) * 2]
+
+    channel(0, image_piece)
 
     def spread(source_ref, target_ref):
         for t in range(TILES):
@@ -515,8 +528,9 @@
         pltpu.VMEM((4, DEPTH, DEPTH), F32),
         pltpu.VMEM((7, 4, 16, DEPTH), F32),
         pltpu.VMEM((4, 16, DEPTH), F32),
-        pltpu.VMEM((3, 16, DEPTH), F32),
-        pltpu.VMEM((9, 16, DEPTH), F32),
+        pltpu.VMEM((2, 4, 4, DEPTH), F32),
+        pltpu.VMEM((3, 4, 16, DEPTH), F32),
+        pltpu.VMEM((2, 3, 4, 4, DEPTH), F32),
         pltpu.VMEM((9, 16, DEPTH), F32),
         pltpu.VMEM((72, DEPTH), F32),
         pltpu.VMEM((TILES * 8, DEPTH), F32),
@@ -534,7 +548,7 @@
         pltpu.VMEM((80, DEPTH), F32),
         dma((len(operands),)),
     ]
-    for count in (8, 3, 7, 8, 7, 3, 8, 21):
+    for count in (8, 3, 7, 8, 7, 35, 21):
         scratch += [dma((count,)), dma((count,))]
     next_wave, new_velocity, moves = pl.pallas_call(
         kernel,

time: 71.3 us -> 68.1 us (0.955)
  Pallas kernels: 69.7 us -> 66.2 us
    pallas_call x1, Pallas kernels: 67.5 us -> 64 us  [shards(): pl.pallas_call(kernel, out_shape=(jax.ShapeDtypeStruct(wave_now.shape, BF...]
where the time goes in v3:
time: 68.1 us; the launch traced here: 67.5 us
  Pallas kernels  66.2 us (97%)
  between operations  1.29 us (2%)
    pallas_call x1, Pallas kernels, shards(): pl.pallas_call(kernel, out_shape=(jax.ShapeDtypeStruct(wave_now.shape, BF...  64 us
    pallas_call x1, Pallas kernels, shards(): pl.pallas_call(writer, out_shape=outs, in_specs=[hbm, hbm, hbm], out_spec...  2.15 us

profile of v3, /device:TPU:1, one launch (start us, length us, event | category | flops | bytes accessed | tf_op | source)
XLA Modules:
  0.0 67.5 jit_solution(1023005965622601136)
XLA Ops:
  1.3 64.0 %shard_map.181 = (bf16[1,8,64,128]{3,2,1,0:T(8,128)(2,1)}, f32[8,2,128]{2,1,0:T(2,128)}, f32[16,128]{1,0:T(8,128)}) custom-call(bf16[1,8,64,128]{3,2,1,0:T(8,128)(2,1)} %wb_in.1, bf16[1,8,64,128]{3,2,1,0:T(8,128)(2,1)} %wn_in.1, bf16[1,8,64,128]{3,2,1,0:T(8,128)(2,1)} %ab_in.1, bf16[1,8,64,128]{3,2,1,0:T(8,128)(2,1)} %an_in.1, f32[8,2,128]{2,1,0:T(2,128)} %vel_in.1, ...), custom_call_target="tpu_custom_call" | custom-call | tf_op jit(solution)/shard_map/pallas_call | solution.py:553
  65.3 2.2 %shard_map.182 = (bf16[1,8,64,128]{3,2,1,0:T(8,128)(2,1)}, f32[8,2,128]{2,1,0:T(2,128)}, f32[3,3,3,2,16]{4,3,2,1,0:T(2,128)}, f32[1,16]{1,0:T(1,128)}, f32[3,3,3,1,16]{4,3,2,1,0:T(1,128)}, /*index=5*/f32[1,1]{1,0:T(1,128)}) custom-call(bf16[1,8,64,128]{3,2,1,0:T(8,128)(2,1)} %get-tuple-element.15.nw, f32[8,2,128]{2,1,0:T(2,128)} %get-tuple-element.16.nv, ...), custom_call_target="tpu_custom_call" | custom-call | tf_op jit(solution)/shard_map/pallas_call | solution.py:575

commit v4 on v3

--- a/solution.py
+++ b/solution.py
@@ -28,6 +28,7 @@
 WIDE = 12
 HID = 48 * DEPTH
 CHUNK = 8 * DEPTH
+FAR_FIRST = (4, 3, 5, 2, 6, 1, 7)
 OFFSETS = tuple(dy * WIDE + dx for dx in range(3) for dy in range(3))
 BLOCKS = 10
 
@@ -95,10 +96,6 @@
     twin = (shot, lax.rem(sub + 8, N_SUB))
     greeted = [xc_peer(k) for k in range(1, 8)] + [zh_peer(k) for k in range(1, 4)] + [twin]
     greeted += [near(d, e) for d, e in around]
-    barrier = pltpu.get_barrier_semaphore()
-    for device in greeted:
-        pl.semaphore_signal(barrier, inc=1, device_id=device, device_id_type=MESH)
-
     loads = [
         pltpu.make_async_copy(outer, inner, s_in.at[n])
         for n, (outer, inner) in enumerate((
@@ -107,7 +104,11 @@
             (b1_in, b1), (k2_in, k2_own), (b2_in, b2),
         ))
     ]
-    for copy in loads:
+    loads[0].start()
+    barrier = pltpu.get_barrier_semaphore()
+    for device in greeted:
+        pl.semaphore_signal(barrier, inc=1, device_id=device, device_id_type=MESH)
+    for copy in loads[1:]:
         copy.start()
 
     pending = []
@@ -233,7 +234,7 @@
     for copy in v1:
         copy.wait_recv()
     v2 = [
-        send(vg.at[:, own, :], vg.at[:, own, :], s_v2.at[k - 1], r_v2.at[k - 1], xc_peer(k)) for k in range(1, 8)
+        send(vg.at[:, own, :], vg.at[:, own, :], s_v2.at[k - 1], r_v2.at[k - 1], xc_peer(k)) for k in FAR_FIRST
     ]
 
     halo_q0 = halo(q0, 2)
@@ -266,9 +267,9 @@
     halo_p1 = halo(p1, 4)
     q1[4:12, every, :] = q1[4:12, every, :] + vfull[...] * lapq[...]
     halo_q1 = halo(q1, 6)
+
+    halo_wait(p1, halo_p1)
     hv = around_sends(hb_vel, s_hv, r_hv)
-
-    halo_wait(p1, halo_p1)
 
     def forward_1(i, carry):
         center, lap = lap_row(p1, i)
@@ -292,13 +293,13 @@
         for i in range(ROWS):
             imgt.at[z][pl.ds(i, 16, stride=8), :] = imgacc[i, z * 16 : (z + 1) * 16, :]
 
-    sends_a = [
-        send(
+    sends_a = {
+        k: send(
             imgt.at[:, pl.ds(pl.multiple_of(lax.rem(xc + k, 8) * 16, 16), 16), :], ra.at[k - 1],
             s_a.at[k - 1], r_a.at[k - 1], xc_peer(k),
         )
-        for k in range(1, 8)
-    ]
+        for k in FAR_FIRST
+    }
     settle(7)
 
     for copy in loads[9:]:
@@ -362,7 +363,7 @@
 
     total = imgt[:, own, :]
     for k in range(1, 8):
-        sends_a[k - 1].wait_recv()
+        sends_a[k].wait_recv()
         total = total + ra[k - 1]
     acca[...] = total
     for side, first in enumerate((0, 6)):
@@ -467,7 +468,7 @@
             send(
                 re.at[level, me], re.at[level, me], s_e.at[level * 7 + k - 1], r_e.at[level * 7 + k - 1], peer(k)
             )
-            for k in range(1, 8)
+            for k in FAR_FIRST
         ]
         settle(7)
         for copy in copies:

time: 68.1 us -> 67.8 us (level)
  no operation moved by 1% of the time
where the time goes in v4:
time: 67.8 us; the launch traced here: 67.4 us
  Pallas kernels  66.1 us (97%)
  between operations  1.29 us (2%)
    pallas_call x1, Pallas kernels, shards(): pl.pallas_call(kernel, out_shape=(jax.ShapeDtypeStruct(wave_now.shape, BF...  63.9 us
    pallas_call x1, Pallas kernels, shards(): pl.pallas_call(writer, out_shape=outs, in_specs=[hbm, hbm, hbm], out_spec...  2.15 us

profile of v4, /device:TPU:1, one launch (start us, length us, event | category | flops | bytes accessed | tf_op | source)
XLA Modules:
  0.0 67.4 jit_solution(1320421175233741866)
XLA Ops:
  1.3 63.9 %shard_map.181 = (bf16[1,8,64,128]{3,2,1,0:T(8,128)(2,1)}, f32[8,2,128]{2,1,0:T(2,128)}, f32[16,128]{1,0:T(8,128)}) custom-call(bf16[1,8,64,128]{3,2,1,0:T(8,128)(2,1)} %wb_in.1, bf16[1,8,64,128]{3,2,1,0:T(8,128)(2,1)} %wn_in.1, bf16[1,8,64,128]{3,2,1,0:T(8,128)(2,1)} %ab_in.1, bf16[1,8,64,128]{3,2,1,0:T(8,128)(2,1)} %an_in.1, f32[8,2,128]{2,1,0:T(2,128)} %vel_in.1, ...), custom_call_target="tpu_custom_call" | custom-call | tf_op jit(solution)/shard_map/pallas_call | solution.py:554
  65.2 2.2 %shard_map.182 = (bf16[1,8,64,128]{3,2,1,0:T(8,128)(2,1)}, f32[8,2,128]{2,1,0:T(2,128)}, f32[3,3,3,2,16]{4,3,2,1,0:T(2,128)}, f32[1,16]{1,0:T(1,128)}, f32[3,3,3,1,16]{4,3,2,1,0:T(1,128)}, /*index=5*/f32[1,1]{1,0:T(1,128)}) custom-call(bf16[1,8,64,128]{3,2,1,0:T(8,128)(2,1)} %get-tuple-element.15.nw, f32[8,2,128]{2,1,0:T(2,128)} %get-tuple-element.16.nv, ...), custom_call_target="tpu_custom_call" | custom-call | tf_op jit(solution)/shard_map/pallas_call | solution.py:576

commit v5 on v4

--- a/solution.py
+++ b/solution.py
@@ -57,8 +57,8 @@
 
 def kernel(
     wb_in, wn_in, ab_in, an_in, vel_in, tgt_in, scell_in, swave_in, rcell_in, rtrace_in, w1_in, b1_in, k2_in, b2_in,
-    nw, nv, moves,
-    wb, wn, ab, an, vel, tgt, scell, swave, rcell, rtrace, w1_own, b1, k2_own, b2,
+    nw_out, nv_out, moves,
+    nw, nv, s_out, wb, wn, ab, an, vel, tgt, scell, swave, rcell, rtrace, w1_own, b1, k2_own, b2,
     p0, q0, p1, q1, lap0, lapq, imgacc, vfull, vg, surf, imgt, ra, acca, edge, whole, sides, hb_vel,
     ext, gs, g2, rs, r2, fhi, flo, hid, smat, tt, mask, re, wt, kt,
     s_in, s_hal, r_hal, s_v1, r_v1, s_v2, r_v2, s_hv, r_hv, s_a, r_a, s_b, r_b, s_e, r_e,
@@ -279,6 +279,8 @@
         return carry
 
     lax.fori_loop(0, ROWS, forward_1, 0)
+    stores = [pltpu.make_async_copy(nw, nw_out, s_out.at[0]), pltpu.make_async_copy(nv, nv_out, s_out.at[1])]
+    stores[0].start()
 
     halo_wait(q1, halo_q1)
 
@@ -432,6 +434,8 @@
         for dz in range(3):
             rs[pl.ds(((j + 2) * WIDE + 2) * 8 + dz, 8, stride=8), :] = shifted(slope, 1 - dz)
 
+    stores[1].start()
+
     spread(rs, r2)
     offsets_r = tuple((2 - dy) * WIDE + (2 - dx) for dx in range(3) for dy in range(3)) + (0,)
     grad_1 = jnp.zeros((32, 160), F32)
@@ -480,6 +484,8 @@
     squares = jnp.sum(jnp.sum(pack * pack, axis=0, keepdims=True), axis=1, keepdims=True)
     factor = 1.0 / jnp.sqrt(squares * (1.0 / ENTRIES) + 1e-06)
     moves[...] = pack * factor
+    for copy in stores:
+        copy.wait()
 
     settle()
 
@@ -522,7 +528,8 @@
     dma = pltpu.SemaphoreType.DMA
     field = pltpu.VMEM((16, COLS + 2 * PAD, DEPTH), F32)
     block = pltpu.VMEM((ROWS, COLS, DEPTH), F32)
-    scratch = [pltpu.VMEM(x.shape, x.dtype) for x in operands[:-1]] + [pltpu.SMEM((1,), F32)] + [
+    scratch = [pltpu.VMEM(wave_now.shape, BF16), pltpu.VMEM(velocity.shape, F32), dma((2,))]
+    scratch += [pltpu.VMEM(x.shape, x.dtype) for x in operands[:-1]] + [pltpu.SMEM((1,), F32)] + [
         field, field, field, field, block, block, block, block,
         pltpu.VMEM((4, DEPTH, DEPTH), F32),
         pltpu.VMEM((COLS, DEPTH), F32),
@@ -559,7 +566,7 @@
             jax.ShapeDtypeStruct((16, DEPTH), F32),
         ),
         in_specs=[hbm] * len(operands),
-        out_specs=(vmem, vmem, vmem),
+        out_specs=(hbm, hbm, vmem),
         scratch_shapes=scratch,
         compiler_params=pltpu.CompilerParams(
             collective_id=0, has_side_effects=True, vmem_limit_bytes=60 * 1024 * 1024

time: 67.8 us -> 67.8 us (level)
  no operation moved by 1% of the time
where the time goes in v5:
time: 67.8 us; the launch traced here: 67.3 us
  Pallas kernels  66 us (97%)
  between operations  1.29 us (2%)
    pallas_call x1, Pallas kernels, shards(): pl.pallas_call(kernel, out_shape=(jax.ShapeDtypeStruct(wave_now.shape, BF...  63.9 us
    pallas_call x1, Pallas kernels, shards(): pl.pallas_call(writer, out_shape=outs, in_specs=[hbm, hbm, hbm], out_spec...  2.15 us

profile of v5, /device:TPU:1, one launch (start us, length us, event | category | flops | bytes accessed | tf_op | source)
XLA Modules:
  0.0 67.3 jit_solution(6271902419084983884)
XLA Ops:
  1.3 63.9 %shard_map.181 = (bf16[1,8,64,128]{3,2,1,0:T(8,128)(2,1)}, f32[8,2,128]{2,1,0:T(2,128)}, f32[16,128]{1,0:T(8,128)}) custom-call(bf16[1,8,64,128]{3,2,1,0:T(8,128)(2,1)} %wb_in.1, bf16[1,8,64,128]{3,2,1,0:T(8,128)(2,1)} %wn_in.1, bf16[1,8,64,128]{3,2,1,0:T(8,128)(2,1)} %ab_in.1, bf16[1,8,64,128]{3,2,1,0:T(8,128)(2,1)} %an_in.1, f32[8,2,128]{2,1,0:T(2,128)} %vel_in.1, ...), custom_call_target="tpu_custom_call" | custom-call | tf_op jit(solution)/shard_map/pallas_call | solution.py:561
  65.2 2.2 %shard_map.182 = (bf16[1,8,64,128]{3,2,1,0:T(8,128)(2,1)}, f32[8,2,128]{2,1,0:T(2,128)}, f32[3,3,3,2,16]{4,3,2,1,0:T(2,128)}, f32[1,16]{1,0:T(1,128)}, f32[3,3,3,1,16]{4,3,2,1,0:T(1,128)}, /*index=5*/f32[1,1]{1,0:T(1,128)}) custom-call(bf16[1,8,64,128]{3,2,1,0:T(8,128)(2,1)} %get-tuple-element.15.nw, f32[8,2,128]{2,1,0:T(2,128)} %get-tuple-element.16.nv, ...), custom_call_target="tpu_custom_call" | custom-call | tf_op jit(solution)/shard_map/pallas_call | solution.py:583
